TPU v7x, 512 devices: a whole 4x8x8 slice. The times are simulated.
512 devices in a mesh: lag: 16 (over x, y_lo, core), row: 32 (over y_hi, z).
Axes of the slice: x: 4, y: 8 (y_hi: 4, y_lo: 2; y = y_hi * 2 + y_lo), z: 8, core: 2. Of those that a mesh axis runs over, the one named last changes fastest.
Arguments:
- currents: bfloat16 [2048, 4096], P('lag', 'row'), may hold values from -6 to 6
- panels: bfloat16 [16, 4096, 4096], P('lag', 'row'), may hold values from -0.09375 to 0.09375
- excitation: float32 [2048, 4096], P('lag', 'row'), may hold values from -6 to 6
Outputs:
- residual: float32 [2048, 4096], P('lag', 'row')
All inputs are finite; a program needn't handle non-finite values.
Results may differ from a plain program's by a relative error of at most 0.0003.
Values may be sent and summed in bfloat16 or wider, within the bound.
No kernel may reach another device: no remote copies, remote signals or barrier semaphores. Data moves between devices by JAX's collectives and lax.ppermute only.
A program may use at most 64 MiB of HBM per device.

v0:
```python
import jax
import jax.numpy as jnp
from jax import lax
from jax.sharding import PartitionSpec as P


def body(currents, panels, excitation):
    gathered = lax.all_gather(currents, "row", axis=1, tiled=True)
    block_len = currents.shape[0]
    row_count = panels.shape[1]
    lag_total = lax.axis_size("lag")
    lag_index = lax.axis_index("lag")
    per_device = panels.shape[0]
    all_times = block_len * lag_total
    start_state = jnp.zeros((all_times + lag_total * per_device, row_count), jnp.float32)
    running = start_state
    matrix = panels[0]
    product = lax.dot_general(
        lax.all_gather(gathered, "lag", axis=0, tiled=True),
        matrix,
        (((1,), (1,)), ((), ())),
        preferred_element_type=jnp.float32,
    )
    position = lag_index * per_device + 0
    running = lax.dynamic_update_slice_in_dim(running, product, position, 0)
    field = lax.psum_scatter(running[:all_times], "lag", scatter_dimension=0, tiled=True)
    return excitation - field


def solution(mesh):
    return jax.shard_map(
        body,
        mesh=mesh,
        in_specs=(P("lag", "row"), P("lag", "row", None), P("lag", "row")),
        out_specs=P("lag", "row"),
        check_vma=False,
    )
```

profile of v0, /device:TPU:1, one launch (start us, length us, event | category | flops | bytes accessed | tf_op | source)
XLA Modules:
  0.0 277.7 jit_solution(599869451686104882)
XLA Ops:
  6.5 0.0 copy-start
  6.5 0.0 copy-start.1
  6.5 0.0 all-gather.3.cloned.1.call-start
  6.5 0.7 all-gather.3.cloned.1.call-update
  7.3 0.0 all-gather.5.cloned.1.call-start
  7.3 84.6 %all-gather.3.cloned.1.call-done = bf16[128,4096]{1,0:T(8,128)(2,1)} async-done(((bf16[128,128]{1,0:T(8,128)(2,1)}), bf16[128,4096]{1,0:T(8,128)(2,1)}) %all-gather.3.cloned.1.call-update) | async-done | bytes 1048592 | tf_op jit(solution)/shard_map/all_gather | solution.py:8
  91.9 0.0 all-gather.5.cloned.1.call-update
  91.9 0.0 reduce-scatter.2.cloned.1.call-start
  92.0 99.4 %all-gather.5.cloned.1.call-done = bf16[2048,4096]{1,0:T(8,128)(2,1)} async-done(((bf16[128,4096]{1,0:T(8,128)(2,1)}), bf16[2048,4096]{1,0:T(8,128)(2,1)}) %all-gather.5.cloned.1.call-update) | async-done | bytes 16777232 | tf_op jit(solution)/shard_map/all_gather | solution.py:19
  191.4 0.0 copy-done
  191.4 8.1 %fusion = f32[2048,128]{1,0:T(8,128)S(1)} fusion(bf16[2048,4096]{1,0:T(8,128)(2,1)} %all-gather.5.cloned.1.call-done, bf16[1,128,4096]{2,1,0:T(8,128)(2,1)S(1)} %copy-done), kind=kOutput, calls=%fused_computation | convolution fusion | flops 2147483648 | bytes 18874368 | tf_op jit(solution)/shard_map/dot_general | solution.py:18
  199.6 0.1 broadcast_in_dim.3
  199.6 4.0 %dynamic_update_slice.3 = f32[2064,128]{1,0:T(8,128)S(1)} dynamic-update-slice(f32[2064,128]{1,0:T(8,128)S(1)} %broadcast_in_dim.3, f32[2048,128]{1,0:T(8,128)S(1)} %fusion, s32[]{:T(128)S(6)} %select_n.3, s32[]{:T(128)} %constant.10.clone.1) | dynamic-update-slice | bytes 2097156 | tf_op jit(solution)/shard_map/dynamic_update_slice | solution.py:25
  203.6 1.0 slice.4
  204.7 0.0 reduce-scatter.2.cloned.1.call-update
  204.7 65.0 %reduce-scatter.2.cloned.1.call-done = f32[128,128]{1,0:T(8,128)} async-done(((f32[2048,128]{1,0:T(8,128)}), f32[128,128]{1,0:T(8,128)}) %reduce-scatter.2.cloned.1.call-update) | async-done | bytes 65552 | tf_op jit(solution)/shard_map/reduce_scatter | solution.py:26
  269.7 0.0 copy-done.1
  269.7 1.5 sub.3
Async XLA Ops:
  6.5 184.9 %copy-start = (bf16[1,128,4096]{2,1,0:T(8,128)(2,1)S(1)}, bf16[1,128,4096]{2,1,0:T(8,128)(2,1)}, u32[]{:S(2)}) copy-start(bf16[1,128,4096]{2,1,0:T(8,128)(2,1)} %param.4) | copy-start | bytes 3145732
  6.5 263.1 %copy-start.1 = (f32[128,128]{1,0:T(8,128)S(1)}, f32[128,128]{1,0:T(8,128)}, u32[]{:S(2)}) copy-start(f32[128,128]{1,0:T(8,128)} %param.5) | copy-start | bytes 196612
  6.5 85.4 %all-gather.3.cloned.1.call-start = ((), (), s32[]{:S(2)}) async-start(), calls=%async_computation.1 | async-start | bytes 1081344 | tf_op jit(solution)/shard_map/all_gather | solution.py:8
  7.3 184.2 %all-gather.5.cloned.1.call-start = ((), (), s32[]{:S(2)}) async-start(), calls=%async_computation.2 | async-start | bytes 17825792 | tf_op jit(solution)/shard_map/all_gather | solution.py:19
  91.9 177.7 %reduce-scatter.2.cloned.1.call-start = ((), (), s32[]{:S(2)}) async-start(), calls=%async_computation.3 | async-start | bytes 1114112 | tf_op jit(solution)/shard_map/reduce_scatter | solution.py:26
Sparse Core Ops, SparseCore 0:
  10.4 81.4 all-gather.2
  94.0 97.3 all-gather.4
  204.8 64.8 reduce-scatter.1
where the time goes:
time: 279 us; the launch traced here: 278 us
  waiting for transfers between devices  250 us (90%)
  between operations  13.1 us (5%)
  matrix products  8.12 us (3%)
  local copies, waits for them, and re-layouts  5.1 us (2%)
    all_gather x1, waiting for transfers between devices, body(): lax.all_gather(gathered, 'lag', axis=0, tiled=True)  99.4 us
    all_gather x1, waiting for transfers between devices, body(): gathered = lax.all_gather(currents, 'row', axis=1, tiled=True)  84.6 us
    reduce_scatter x1, waiting for transfers between devices, body(): lax.psum_scatter(running[:all_times], 'lag', scatter_dimension=0, tiled=T...  65 us
    dot_general x1, matrix products, body(): lax.dot_general(lax.all_gather(gathered, 'lag', axis=0, tiled=True), matr...  8.12 us
  transfers between devices with their start and end apart: 3, of which 3 were waited for; matrix products, arithmetic and copies ran while one was open for 0% of the time, Pallas kernels for 0%

commit v1 on v0

v1 whole, which is shorter than its diff:
```python
import jax
import jax.numpy as jnp
from jax import lax
from jax.experimental import pallas as pl
from jax.experimental.pallas import tpu as pltpu
from jax.sharding import Mesh, PartitionSpec as P

B = 128
HALO = 16
LAGS = 16
LAG = ("x", "yl", "c")
ROW = ("yh", "zh", "zl")
TRADE = ("x", "yl", "zl")
COPIES = ("yh", "zh")


def swap_pairs():
    pairs = []
    for x in range(4):
        for yl in range(2):
            for c in range(2):
                for yh in range(4):
                    for zh in range(4):
                        for zl in range(2):
                            src = ((x * 2 + yl) * 2 + c) * 32 + yh * 8 + zh * 2 + zl
                            to_z = (zh // 2) * 2 + yl
                            dst = ((yh * 2 + zh % 2) * 2 + c) * 32 + x * 8 + to_z * 2 + zl
                            pairs.append((src, dst))
    return pairs


def split_kernel(p_ref, o_ref):
    for x in range(4):
        for yl in range(2):
            for zl in range(2):
                for h in range(2):
                    col = (x * 8 + h * 4 + yl * 2 + zl) * B
                    o_ref[(x * 2 + yl) * 2 + zl, :, h * B:(h + 1) * B] = p_ref[0, :, col:col + B]


def split_panels(panels):
    vmem = pl.BlockSpec(memory_space=pltpu.VMEM)
    return pl.pallas_call(
        split_kernel,
        out_shape=jax.ShapeDtypeStruct((16, B, 2 * B), jnp.bfloat16),
        in_specs=[vmem],
        out_specs=vmem,
        name="split",
    )(panels)


def field_kernel(c_ref, own_ref, other_ref, x_ref, out_ref, w_ref, a_ref):
    core = c_ref[0]
    for k in range(8):
        w_ref[2 * k + core] = own_ref[k]
        w_ref[2 * k + 1 - core] = other_ref[k]
    for m in range(8):
        for h in range(2):
            slab = x_ref[(m // 2) * 4 + h * 2 + m % 2].astype(jnp.float32)
            for k in range(LAGS):
                a_ref[m * B:(m + 1) * B, (2 * k + h) * B:(2 * k + h + 1) * B] = slab[HALO - k:HALO - k + B].astype(jnp.bfloat16)
    for s in range(2):
        acc = jnp.zeros((4 * B, 2 * B), jnp.float32)
        for k in range(LAGS):
            acc += lax.dot_general(
                a_ref[s * 4 * B:(s + 1) * 4 * B, k * 2 * B:(k + 1) * 2 * B], w_ref[k], (((1,), (1,)), ((), ())), preferred_element_type=jnp.float32
            )
        for m in range(4):
            for zl in range(2):
                out_ref[(s * 4 + m) * 2 + zl] = acc[m * B:(m + 1) * B, zl * B:(zl + 1) * B].astype(out_ref.dtype)


def field_of(core, own, other, x):
    vmem = pl.BlockSpec(memory_space=pltpu.VMEM)
    return pl.pallas_call(
        field_kernel,
        out_shape=jax.ShapeDtypeStruct((16, B, B), jnp.float32),
        in_specs=[pl.BlockSpec(memory_space=pltpu.SMEM), vmem, vmem, vmem],
        out_specs=vmem,
        scratch_shapes=[
            pltpu.VMEM((LAGS, 2 * B, 2 * B), jnp.bfloat16),
            pltpu.VMEM((8 * B, LAGS * 2 * B), jnp.bfloat16),
        ],
        compiler_params=pltpu.CompilerParams(vmem_limit_bytes=48 * 1024 * 1024),
        name="field",
    )(core, own, other, x)


def body(currents, panels, excitation):
    halo = lax.ppermute(currents[B - HALO:], LAG, [(i, i + 1) for i in range(15)])
    piece = jnp.concatenate([halo, currents], 0)
    own = lax.all_to_all(split_panels(panels), TRADE, 0, 0, tiled=True).reshape(8, 2 * B, 2 * B)
    piece = lax.ppermute(piece, LAG + ROW, swap_pairs())
    x = lax.all_to_all(jnp.broadcast_to(piece[None], (16,) + piece.shape), COPIES, 0, 0, tiled=True)
    other = lax.ppermute(own, "c", [(0, 1), (1, 0)])
    core = lax.axis_index("c").astype(jnp.int32).reshape(1)
    part = field_of(core, own, other, x).astype(jnp.float16)
    got = lax.all_to_all(part, TRADE, 0, 0, tiled=True)
    return excitation - jnp.sum(got.astype(jnp.float32), 0)


def solution(mesh):
    fine = Mesh(mesh.devices.reshape(4, 2, 2, 4, 4, 2), LAG + ROW)
    return jax.shard_map(
        body,
        mesh=fine,
        in_specs=(P(LAG, ROW), P(LAG, ROW, None), P(LAG, ROW)),
        out_specs=P(LAG, ROW),
        check_vma=False,
    )
```

time: 279 us -> 88.8 us (0.32)
  waiting for transfers between devices: 250 us -> 20.2 us
  starting transfers between devices: 0.08 us -> 41.1 us
  blocking collectives: 0 us -> 18.1 us
  between operations: 13.1 us -> 0.09 us
  matrix products: 8.12 us -> 0 us
  Pallas kernels: 0 us -> 6.2 us
  local copies, waits for them, and re-layouts: 5.1 us -> 1.67 us
    all_gather x2 -> x0, waiting for transfers between devices: 184 us -> none  [the longest x1 99.4 us: body(): lax.all_gather(gathered, 'lag', axis=0, tiled=True)]
    reduce_scatter x1 -> x0, waiting for transfers between devices: 65 us -> none  [body(): lax.psum_scatter(running[:all_times], 'lag', scatter_dimension=0, tiled=T...]
    all_to_all x0 -> x2, starting transfers between devices: none -> 32.4 us  [the longest x1 24.5 us: body(): lax.all_to_all(jnp.broadcast_to(piece[None], (16,) + piece.shape), COPIES...]
    all_to_all x0 -> x1, blocking collectives: none -> 18.1 us  [body(): got = lax.all_to_all(part, TRADE, 0, 0, tiled=True)]
    all_to_all x0 -> x2, waiting for transfers between devices: none -> 17.3 us  [the longest x1 13.9 us: body(): lax.all_to_all(jnp.broadcast_to(piece[None], (16,) + piece.shape), COPIES...]
    ppermute x0 -> x3, starting transfers between devices: none -> 8.65 us  [the longest x1 6.08 us: body(): lax.ppermute(currents[B - HALO:], LAG, [(i, i + 1) for i in range(15)])]
    dot_general x1 -> x0, matrix products: 8.12 us -> none  [body(): lax.dot_general(lax.all_gather(gathered, 'lag', axis=0, tiled=True), matr...]
    pallas_call x0 -> x2, Pallas kernels: none -> 6.2 us  [the longest x1 3.83 us: field_of(): pl.pallas_call(field_kernel, out_shape=jax.ShapeDtypeStruct((16, B, B), j...]
  transfers between devices with their start and end apart: 3 -> 5, of which waited for: 3 -> 3; matrix products, arithmetic and copies ran while one was open for 0% -> 0% of each run, Pallas kernels for 0% -> 0%
where the time goes in v1:
time: 88.8 us; the launch traced here: 88.1 us
  starting transfers between devices  41.1 us (46%)
  waiting for transfers between devices  20.2 us (23%)
  blocking collectives  18.1 us (20%)
  Pallas kernels  6.2 us (7%)
  local copies, waits for them, and re-layouts  1.67 us (2%)
    all_to_all x1, starting transfers between devices, body(): lax.all_to_all(jnp.broadcast_to(piece[None], (16,) + piece.shape), COPIES...  24.5 us
    all_to_all x1, blocking collectives, body(): got = lax.all_to_all(part, TRADE, 0, 0, tiled=True)  18.1 us
    all_to_all x1, waiting for transfers between devices, body(): lax.all_to_all(jnp.broadcast_to(piece[None], (16,) + piece.shape), COPIES...  13.9 us
    all_to_all x1, starting transfers between devices, body(): lax.all_to_all(split_panels(panels), TRADE, 0, 0, tiled=True)  7.91 us
    ppermute x1, starting transfers between devices, body(): lax.ppermute(currents[B - HALO:], LAG, [(i, i + 1) for i in range(15)])  6.08 us
    pallas_call x1, Pallas kernels, field_of(): pl.pallas_call(field_kernel, out_shape=jax.ShapeDtypeStruct((16, B, B), j...  3.83 us
    all_to_all x1, waiting for transfers between devices, body(): lax.all_to_all(split_panels(panels), TRADE, 0, 0, tiled=True)  3.42 us
    ppermute x1, waiting for transfers between devices, body(): lax.ppermute(currents[B - HALO:], LAG, [(i, i + 1) for i in range(15)])  2.86 us
  transfers between devices with their start and end apart: 5, of which 3 were waited for; matrix products, arithmetic and copies ran while one was open for 0% of the time, Pallas kernels for 0%

profile of v1, /device:TPU:1, one launch (start us, length us, event | category | flops | bytes accessed | tf_op | source)
XLA Modules:
  0.0 88.1 jit_solution(15442288140132547796)
XLA Ops:
  0.0 2.4 %split.1 = bf16[16,128,256]{2,1,0:T(8,128)(2,1)} custom-call(bf16[1,128,4096]{2,1,0:T(8,128)(2,1)} %p_ref.1), custom_call_target="tpu_custom_call" | custom-call | tf_op jit(solution)/shard_map/split/pallas_call | solution.py:43
  2.4 0.0 copy-start.1
  2.4 7.9 %all-to-all-start = ((bf16[16,128,256]{2,1,0:T(8,128)(2,1)}), bf16[16,128,256]{2,1,0:T(8,128)(2,1)S(1)}, u32[]{:S(2)}, u32[]{:S(2)}) async-start(bf16[16,128,256]{2,1,0:T(8,128)(2,1)} %split.1), calls=%async_computation | async-start | bytes 2097152 | tf_op jit(solution)/shard_map/all_to_all | solution.py:92
  10.3 0.0 copy-done.1
  10.3 6.1 %collective-permute-start.1 = (bf16[16,128]{1,0:T(8,128)(2,1)S(1)}, bf16[16,128]{1,0:T(8,128)(2,1)S(1)}, u32[]{:S(2)}, u32[]{:S(2)}) collective-permute-start(bf16[16,128]{1,0:T(8,128)(2,1)S(1)} %slice.3), channel_id=1, source_target_pairs={{0,32},{32,64},{64,96},{96,128},{128,160},{160,192},{192,224},{224... | collective-permute-start | bytes 12296 | tf_op jit(solution)/shard_map/ppermute | solution.py:90
  16.4 2.9 %collective-permute-done.1 = bf16[16,128]{1,0:T(8,128)(2,1)S(1)} collective-permute-done((bf16[16,128]{1,0:T(8,128)(2,1)S(1)}, bf16[16,128]{1,0:T(8,128)(2,1)S(1)}, u32[]{:S(2)}, u32[]{:S(2)}) %collective-permute-start.1) | collective-permute-done | bytes 4128 | tf_op jit(solution)/shard_map/ppermute | solution.py:90
  19.3 0.7 collective-permute-start.2
  19.9 0.0 collective-permute-done.2
  19.9 3.4 %all-to-all-done = bf16[16,128,256]{2,1,0:T(8,128)(2,1)S(1)} async-done(((bf16[16,128,256]{2,1,0:T(8,128)(2,1)}), bf16[16,128,256]{2,1,0:T(8,128)(2,1)S(1)}, u32[]{:S(2)}, u32[]{:S(2)}) %all-to-all-start) | async-done | bytes 1048608 | tf_op jit(solution)/shard_map/all_to_all | solution.py:92
  23.4 0.9 %broadcast_in_dim.2 = bf16[16,144,128]{2,1,0:T(8,128)(2,1)} broadcast(bf16[144,128]{1,0:T(8,128)(2,1)S(1)} %collective-permute-done.2), dimensions={1,2} | broadcast | bytes 626688 | tf_op jit(solution)/shard_map/broadcast_in_dim | solution.py:94
  24.2 24.5 %all-to-all-start.1 = ((bf16[16,144,128]{2,1,0:T(8,128)(2,1)}), bf16[16,144,128]{2,1,0:T(8,128)(2,1)S(1)}, u32[]{:S(2)}, u32[]{:S(2)}) async-start(bf16[16,144,128]{2,1,0:T(8,128)(2,1)} %broadcast_in_dim.2), calls=%async_computation.1 | async-start | bytes 1179648 | tf_op jit(solution)/shard_map/all_to_all | solution.py:94
  48.8 1.9 %collective-permute-start = (bf16[8,256,256]{2,1,0:T(8,128)(2,1)S(1)}, bf16[8,256,256]{2,1,0:T(8,128)(2,1)S(1)}, u32[]{:S(2)}, u32[]{:S(2)}) collective-permute-start(bf16[8,256,256]{2,1,0:T(8,128)(2,1)S(1)} %bitcast.2), channel_id=1, source_target_pairs={{0,32},{32,0},{1,33},{33,1},{2,34},{34,2},{3,35},{35,3},{4,36},{36... | collective-permute-start | bytes 3145736 | tf_op jit(solution)/shard_map/ppermute | solution.py:95
  50.7 13.9 %all-to-all-done.1.x_ref = bf16[16,144,128]{2,1,0:T(8,128)(2,1)S(1)} async-done(((bf16[16,144,128]{2,1,0:T(8,128)(2,1)}), bf16[16,144,128]{2,1,0:T(8,128)(2,1)S(1)}, u32[]{:S(2)}, u32[]{:S(2)}) %all-to-all-start.1) | async-done | bytes 589856 | tf_op jit(solution)/shard_map/all_to_all | solution.py:94
  64.7 0.0 collective-permute-done.other_ref
  64.7 3.8 %field.1 = f32[16,128,128]{2,1,0:T(8,128)S(1)} custom-call(s32[1]{0:T(128)} %bitcast.c_ref, bf16[8,256,256]{2,1,0:T(8,128)(2,1)S(1)} %bitcast.3, bf16[8,256,256]{2,1,0:T(8,128)(2,1)S(1)} %collective-permute-done.other_ref, bf16[16,144,128]{2,1,0:T(8,128)(2,1)S(1)} %all-to-all-done.1.x_ref), custom_call_target="tpu_custom_call" | custom-call | tf_op jit(solution)/shard_map/field/pallas_call | solution.py:75
  68.5 0.1 convert_element_type.6
  68.6 18.1 %all_to_all.15 = f16[16,128,128]{2,1,0:T(8,128)(2,1)S(1)} all-to-all(f16[16,128,128]{2,1,0:T(8,128)(2,1)S(1)} %convert_element_type.6), channel_id=1, replica_groups=mesh['x'=4,'yl'=2,'c'=2,'yh'=4,'zh'=4,'zl'=2] {'x','yl','zl'}, dimensions={0} | all-to-all | bytes 1048576 | tf_op jit(solution)/shard_map/all_to_all | solution.py:98
  86.7 0.0 copy-start
  86.7 0.1 convert_reduce_fusion
  86.7 0.8 copy-done
  87.5 0.6 sub.3
  (2 shorter events, 0.0 us)
Async XLA Ops:
  2.4 7.9 %copy-start.1 = (bf16[128,128]{1,0:T(8,128)(2,1)S(1)}, bf16[128,128]{1,0:T(8,128)(2,1)}, u32[]{:S(2)}) copy-start(bf16[128,128]{1,0:T(8,128)(2,1)} %param.3) | copy-start | bytes 98308
  2.4 21.0 %all-to-all-start = ((bf16[16,128,256]{2,1,0:T(8,128)(2,1)}), bf16[16,128,256]{2,1,0:T(8,128)(2,1)S(1)}, u32[]{:S(2)}, u32[]{:S(2)}) async-start(bf16[16,128,256]{2,1,0:T(8,128)(2,1)} %split.1), calls=%async_computation | async-start | bytes 2097152 | tf_op jit(solution)/shard_map/all_to_all | solution.py:92
  10.3 8.9 %collective-permute-start.1 = (bf16[16,128]{1,0:T(8,128)(2,1)S(1)}, bf16[16,128]{1,0:T(8,128)(2,1)S(1)}, u32[]{:S(2)}, u32[]{:S(2)}) collective-permute-start(bf16[16,128]{1,0:T(8,128)(2,1)S(1)} %slice.3), channel_id=1, source_target_pairs={{0,32},{32,64},{64,96},{96,128},{128,160},{160,192},{192,224},{224... | collective-permute-start | bytes 12296 | tf_op jit(solution)/shard_map/ppermute | solution.py:90
  19.3 0.7 collective-permute-start.2
  24.2 40.4 %all-to-all-start.1 = ((bf16[16,144,128]{2,1,0:T(8,128)(2,1)}), bf16[16,144,128]{2,1,0:T(8,128)(2,1)S(1)}, u32[]{:S(2)}, u32[]{:S(2)}) async-start(bf16[16,144,128]{2,1,0:T(8,128)(2,1)} %broadcast_in_dim.2), calls=%async_computation.1 | async-start | bytes 1179648 | tf_op jit(solution)/shard_map/all_to_all | solution.py:94
  48.8 15.9 %collective-permute-start = (bf16[8,256,256]{2,1,0:T(8,128)(2,1)S(1)}, bf16[8,256,256]{2,1,0:T(8,128)(2,1)S(1)}, u32[]{:S(2)}, u32[]{:S(2)}) collective-permute-start(bf16[8,256,256]{2,1,0:T(8,128)(2,1)S(1)} %bitcast.2), channel_id=1, source_target_pairs={{0,32},{32,0},{1,33},{33,1},{2,34},{34,2},{3,35},{35,3},{4,36},{36... | collective-permute-start | bytes 3145736 | tf_op jit(solution)/shard_map/ppermute | solution.py:95
  86.7 0.8 copy-start

commit v2 on v1

v2 whole, which is shorter than its diff:
```python
import jax
import jax.numpy as jnp
from jax import lax
from jax.experimental import pallas as pl
from jax.experimental.pallas import tpu as pltpu
from jax.sharding import Mesh, PartitionSpec as P

B = 128
HALO = 16
LAGS = 16
LAG = ("x", "yl", "c")
ROW = ("yh", "zh", "zl")
TRADE = ("x", "yl", "zl")
COPIES = ("yh", "zh")


def swap_pairs(step):
    pairs = []
    for lag in range(16 - step):
        for row in range(32):
            x, yl, c = (lag + step) // 4, (lag + step) // 2 % 2, (lag + step) % 2
            yh, zh, zl = row // 8, row // 2 % 4, row % 2
            to_lag = (yh * 2 + zh % 2) * 2 + c
            to_row = x * 8 + (zh // 2 * 2 + yl) * 2 + zl
            pairs.append((lag * 32 + row, to_lag * 32 + to_row))
    return pairs


def split_kernel(p_ref, o_ref, in_ref, out_ref, in_sem, out_sem):
    parts = 4
    rows = B // parts
    loads = [pltpu.make_async_copy(p_ref.at[0, pl.ds(i * rows, rows)], in_ref.at[pl.ds(i * rows, rows)], in_sem.at[i]) for i in range(parts)]
    for load in loads:
        load.start()
    stores = []
    for i in range(parts):
        loads[i].wait()
        here = slice(i * rows, (i + 1) * rows)
        for x in range(4):
            for yl in range(2):
                for zl in range(2):
                    for h in range(2):
                        col = (x * 8 + h * 4 + yl * 2 + zl) * B
                        out_ref[(x * 2 + yl) * 2 + zl, here, h * B:(h + 1) * B] = in_ref[here, col:col + B]
        stores.append(pltpu.make_async_copy(out_ref.at[:, pl.ds(i * rows, rows)], o_ref.at[:, pl.ds(i * rows, rows)], out_sem.at[i]))
        stores[i].start()
    for store in stores:
        store.wait()


def split_panels(panels):
    anywhere = pl.BlockSpec(memory_space=pl.ANY)
    return pl.pallas_call(
        split_kernel,
        out_shape=jax.ShapeDtypeStruct((16, B, 2 * B), jnp.bfloat16),
        in_specs=[anywhere],
        out_specs=anywhere,
        scratch_shapes=[
            pltpu.VMEM((B, 32 * B), jnp.bfloat16),
            pltpu.VMEM((16, B, 2 * B), jnp.bfloat16),
            pltpu.SemaphoreType.DMA((4,)),
            pltpu.SemaphoreType.DMA((4,)),
        ],
        name="split",
    )(panels)


def field_kernel(c_ref, own_ref, other_ref, x_ref, h_ref, e_ref, out_ref, kept_ref, s_ref):
    core = c_ref[0]
    kept_ref[...] = e_ref[...]

    def place(m, h):
        return (m // 2) * 4 + h * 2 + m % 2

    def run(c):
        for m in range(8):
            for h in range(2):
                cols = slice(h * B, (h + 1) * B)
                before = m - 1 + c
                if before < 0:
                    s_ref[m, 0:HALO, cols] = jnp.zeros((HALO, B), jnp.float32)
                else:
                    s_ref[m, 0:HALO, cols] = h_ref[place(before, h)].astype(jnp.float32)
                s_ref[m, HALO:, cols] = x_ref[place(m, h)].astype(jnp.float32)
        acc = jnp.zeros((8 * B, 2 * B), jnp.float32)
        for k in range(LAGS):
            w_ref = own_ref if k % 2 == c else other_ref
            shifted = s_ref[:, HALO - k:HALO - k + B, :].astype(jnp.bfloat16).reshape(8 * B, 2 * B)
            acc += lax.dot_general(shifted, w_ref[k // 2], (((1,), (1,)), ((), ())), preferred_element_type=jnp.float32)
        for m in range(8):
            for zl in range(2):
                out_ref[m * 2 + zl] = acc[m * B:(m + 1) * B, zl * B:(zl + 1) * B]

    pl.when(core == 0)(lambda: run(0))
    pl.when(core == 1)(lambda: run(1))


def field_of(core, own, other, x, ends, excitation):
    vmem = pl.BlockSpec(memory_space=pltpu.VMEM)
    return pl.pallas_call(
        field_kernel,
        out_shape=(jax.ShapeDtypeStruct((16, B, B), jnp.float32), jax.ShapeDtypeStruct((B, B), jnp.float32)),
        in_specs=[pl.BlockSpec(memory_space=pltpu.SMEM)] + [vmem] * 5,
        out_specs=(vmem, vmem),
        scratch_shapes=[pltpu.VMEM((8, HALO + B, 2 * B), jnp.float32)],
        compiler_params=pltpu.CompilerParams(vmem_limit_bytes=48 * 1024 * 1024),
        name="field",
    )(core, own, other, x, ends, excitation)


def body(currents, panels, excitation):
    everyone = LAG + ROW
    own = lax.all_to_all(split_panels(panels), TRADE, 0, 0, tiled=True).reshape(8, 2 * B, 2 * B)
    block = lax.ppermute(currents, everyone, swap_pairs(0))
    x = lax.all_to_all(jnp.broadcast_to(block[None], (16,) + block.shape), COPIES, 0, 0, tiled=True)
    ends = lax.ppermute(x[:, B - HALO:], "c", [(0, 1), (1, 0)])
    other = lax.ppermute(own, "c", [(0, 1), (1, 0)])
    core = lax.axis_index("c").astype(jnp.int32).reshape(1)
    part, kept = field_of(core, own, other, x, ends, excitation)
    got = lax.all_to_all(part.astype(jnp.float16), TRADE, 0, 0, tiled=True)
    return kept - jnp.sum(got.astype(jnp.float32), 0)


def solution(mesh):
    fine = Mesh(mesh.devices.reshape(4, 2, 2, 4, 4, 2), LAG + ROW)
    return jax.shard_map(
        body,
        mesh=fine,
        in_specs=(P(LAG, ROW), P(LAG, ROW, None), P(LAG, ROW)),
        out_specs=P(LAG, ROW),
        check_vma=False,
    )
```

time: 88.8 us -> 83.7 us (0.943)
  starting transfers between devices: 41.1 us -> 34 us
  waiting for transfers between devices: 20.2 us -> 23.4 us
  Pallas kernels: 6.2 us -> 4.4 us
  blocking collectives: 18.1 us -> 19.6 us
    all_to_all x1, waiting for transfers between devices: 3.42 us -> 12.4 us  [body(): lax.all_to_all(split_panels(panels), TRADE, 0, 0, tiled=True)]
    all_to_all x1, starting transfers between devices: 24.5 us -> 15.7 us  [body(): lax.all_to_all(jnp.broadcast_to(block[None], (16,) + block.shape), COPIES...]
    all_to_all x1, waiting for transfers between devices: 13.9 us -> 10.2 us  [body(): lax.all_to_all(jnp.broadcast_to(block[None], (16,) + block.shape), COPIES...]
    ppermute x1, starting transfers between devices: 1.92 us -> 4.46 us  [body(): other = lax.ppermute(own, 'c', [(0, 1), (1, 0)])]
    ppermute x2, waiting for transfers between devices: 2.86 us -> 0.88 us  [the longest x1 0.88 us: body(): ends = lax.ppermute(x[:, B - HALO:], 'c', [(0, 1), (1, 0)])]
    all_to_all x1, blocking collectives: 18.1 us -> 19.6 us  [body(): got = lax.all_to_all(part.astype(jnp.float16), TRADE, 0, 0, tiled=True)]
    pallas_call x1, Pallas kernels: 3.83 us -> 2.37 us  [field_of(): pl.pallas_call(field_kernel, out_shape=(jax.ShapeDtypeStruct((16, B, B),...]
where the time goes in v2:
time: 83.7 us; the launch traced here: 83.3 us
  starting transfers between devices  34 us (41%)
  waiting for transfers between devices  23.4 us (28%)
  blocking collectives  19.6 us (23%)
  Pallas kernels  4.4 us (5%)
  local copies, waits for them, and re-layouts  0.91 us (1%)
    all_to_all x1, blocking collectives, body(): got = lax.all_to_all(part.astype(jnp.float16), TRADE, 0, 0, tiled=True)  19.6 us
    all_to_all x1, starting transfers between devices, body(): lax.all_to_all(jnp.broadcast_to(block[None], (16,) + block.shape), COPIES...  15.7 us
    all_to_all x1, waiting for transfers between devices, body(): lax.all_to_all(split_panels(panels), TRADE, 0, 0, tiled=True)  12.4 us
    all_to_all x1, waiting for transfers between devices, body(): lax.all_to_all(jnp.broadcast_to(block[None], (16,) + block.shape), COPIES...  10.2 us
    all_to_all x1, starting transfers between devices, body(): lax.all_to_all(split_panels(panels), TRADE, 0, 0, tiled=True)  7.79 us
    ppermute x1, starting transfers between devices, body(): ends = lax.ppermute(x[:, B - HALO:], 'c', [(0, 1), (1, 0)])  5.39 us
    ppermute x1, starting transfers between devices, body(): other = lax.ppermute(own, 'c', [(0, 1), (1, 0)])  4.46 us
    pallas_call x1, Pallas kernels, field_of(): pl.pallas_call(field_kernel, out_shape=(jax.ShapeDtypeStruct((16, B, B),...  2.37 us
  transfers between devices with their start and end apart: 5, of which 3 were waited for; matrix products, arithmetic and copies ran while one was open for 0% of the time, Pallas kernels for 0%

profile of v2, /device:TPU:1, one launch (start us, length us, event | category | flops | bytes accessed | tf_op | source)
XLA Modules:
  0.0 83.3 jit_solution(6890684090505309282)
XLA Ops:
  0.0 2.0 %split.1 = bf16[16,128,256]{2,1,0:T(8,128)(2,1)} custom-call(bf16[1,128,4096]{2,1,0:T(8,128)(2,1)} %p_ref.1), custom_call_target="tpu_custom_call" | custom-call | tf_op jit(solution)/shard_map/split/pallas_call | solution.py:53
  2.0 0.0 copy-start.1
  2.1 7.8 %all-to-all-start = ((bf16[16,128,256]{2,1,0:T(8,128)(2,1)}), bf16[16,128,256]{2,1,0:T(8,128)(2,1)S(1)}, u32[]{:S(2)}, u32[]{:S(2)}) async-start(bf16[16,128,256]{2,1,0:T(8,128)(2,1)} %split.1), calls=%async_computation | async-start | bytes 2097152 | tf_op jit(solution)/shard_map/all_to_all | solution.py:113
  9.9 0.0 copy-done.1
  9.9 0.7 collective-permute-start.1
  10.5 0.0 collective-permute-done.1
  10.5 12.4 %all-to-all-done = bf16[16,128,256]{2,1,0:T(8,128)(2,1)S(1)} async-done(((bf16[16,128,256]{2,1,0:T(8,128)(2,1)}), bf16[16,128,256]{2,1,0:T(8,128)(2,1)S(1)}, u32[]{:S(2)}, u32[]{:S(2)}) %all-to-all-start) | async-done | bytes 1048608 | tf_op jit(solution)/shard_map/all_to_all | solution.py:113
  22.9 0.9 %broadcast_in_dim.2 = bf16[16,128,128]{2,1,0:T(8,128)(2,1)} broadcast(bf16[128,128]{1,0:T(8,128)(2,1)S(1)} %collective-permute-done.1), dimensions={1,2} | broadcast | bytes 557056 | tf_op jit(solution)/shard_map/broadcast_in_dim | solution.py:115
  23.8 15.7 %all-to-all-start.1 = ((bf16[16,128,128]{2,1,0:T(8,128)(2,1)}), bf16[16,128,128]{2,1,0:T(8,128)(2,1)S(1)}, u32[]{:S(2)}, u32[]{:S(2)}) async-start(bf16[16,128,128]{2,1,0:T(8,128)(2,1)} %broadcast_in_dim.2), calls=%async_computation.1 | async-start | bytes 1048576 | tf_op jit(solution)/shard_map/all_to_all | solution.py:115
  39.5 0.0 copy-start
  39.5 4.5 %collective-permute-start = (bf16[8,256,256]{2,1,0:T(8,128)(2,1)S(1)}, bf16[8,256,256]{2,1,0:T(8,128)(2,1)S(1)}, u32[]{:S(2)}, u32[]{:S(2)}) collective-permute-start(bf16[8,256,256]{2,1,0:T(8,128)(2,1)S(1)} %bitcast.2), channel_id=1, source_target_pairs={{0,32},{32,0},{1,33},{33,1},{2,34},{34,2},{3,35},{35,3},{4,36},{36... | collective-permute-start | bytes 3145736 | tf_op jit(solution)/shard_map/ppermute | solution.py:117
  44.0 10.2 %all-to-all-done.1.x_ref = bf16[16,128,128]{2,1,0:T(8,128)(2,1)S(1)} async-done(((bf16[16,128,128]{2,1,0:T(8,128)(2,1)}), bf16[16,128,128]{2,1,0:T(8,128)(2,1)S(1)}, u32[]{:S(2)}, u32[]{:S(2)}) %all-to-all-start.1) | async-done | bytes 524320 | tf_op jit(solution)/shard_map/all_to_all | solution.py:115
  54.2 5.4 %collective-permute-start.2 = (bf16[16,16,128]{2,1,0:T(8,128)(2,1)S(1)}, bf16[16,16,128]{2,1,0:T(8,128)(2,1)S(1)}, u32[]{:S(2)}, u32[]{:S(2)}) collective-permute-start(bf16[16,16,128]{2,1,0:T(8,128)(2,1)S(1)} %slice.4), channel_id=1, source_target_pairs={{0,32},{32,0},{1,33},{33,1},{2,34},{34,2},{3,35},{35,3},{4,36},{36... | collective-permute-start | bytes 196616 | tf_op jit(solution)/shard_map/ppermute | solution.py:116
  59.6 0.9 %collective-permute-done.2.h_ref = bf16[16,16,128]{2,1,0:T(8,128)(2,1)S(1)} collective-permute-done((bf16[16,16,128]{2,1,0:T(8,128)(2,1)S(1)}, bf16[16,16,128]{2,1,0:T(8,128)(2,1)S(1)}, u32[]{:S(2)}, u32[]{:S(2)}) %collective-permute-start.2) | collective-permute-done | bytes 65568 | tf_op jit(solution)/shard_map/ppermute | solution.py:116
  60.5 0.0 collective-permute-done.other_ref
  60.5 0.0 copy-done
  60.5 2.4 %field.1 = (f32[16,128,128]{2,1,0:T(8,128)S(1)}, f32[128,128]{1,0:T(8,128)S(1)}) custom-call(s32[1]{0:T(128)} %bitcast.c_ref, bf16[8,256,256]{2,1,0:T(8,128)(2,1)S(1)} %bitcast.3, bf16[8,256,256]{2,1,0:T(8,128)(2,1)S(1)} %collective-permute-done.other_ref, bf16[16,128,128]{2,1,0:T(8,128)(2,1)S(1)} %all-to-all-done.1.x_ref, ...), custom_call_target="tpu_custom_call" | custom-call | tf_op jit(solution)/shard_map/field/pallas_call | solution.py:100
  62.9 0.1 convert_element_type.6
  63.0 19.6 %all_to_all.15 = f16[16,128,128]{2,1,0:T(8,128)(2,1)S(1)} all-to-all(f16[16,128,128]{2,1,0:T(8,128)(2,1)S(1)} %convert_element_type.6), channel_id=1, replica_groups=mesh['x'=4,'yl'=2,'c'=2,'yh'=4,'zh'=4,'zl'=2] {'x','yl','zl'}, dimensions={0} | all-to-all | bytes 1048576 | tf_op jit(solution)/shard_map/all_to_all | solution.py:120
  82.5 0.1 convert_reduce_fusion
  82.6 0.6 sub.3
  (1 shorter events, 0.0 us)
Async XLA Ops:
  2.0 7.8 %copy-start.1 = (bf16[128,128]{1,0:T(8,128)(2,1)S(1)}, bf16[128,128]{1,0:T(8,128)(2,1)}, u32[]{:S(2)}) copy-start(bf16[128,128]{1,0:T(8,128)(2,1)} %param.3) | copy-start | bytes 98308
  2.1 20.9 %all-to-all-start = ((bf16[16,128,256]{2,1,0:T(8,128)(2,1)}), bf16[16,128,256]{2,1,0:T(8,128)(2,1)S(1)}, u32[]{:S(2)}, u32[]{:S(2)}) async-start(bf16[16,128,256]{2,1,0:T(8,128)(2,1)} %split.1), calls=%async_computation | async-start | bytes 2097152 | tf_op jit(solution)/shard_map/all_to_all | solution.py:113
  9.9 0.7 collective-permute-start.1
  23.8 30.4 %all-to-all-start.1 = ((bf16[16,128,128]{2,1,0:T(8,128)(2,1)}), bf16[16,128,128]{2,1,0:T(8,128)(2,1)S(1)}, u32[]{:S(2)}, u32[]{:S(2)}) async-start(bf16[16,128,128]{2,1,0:T(8,128)(2,1)} %broadcast_in_dim.2), calls=%async_computation.1 | async-start | bytes 1048576 | tf_op jit(solution)/shard_map/all_to_all | solution.py:115
  39.5 20.9 %copy-start = (f32[128,128]{1,0:T(8,128)S(1)}, f32[128,128]{1,0:T(8,128)}, u32[]{:S(2)}) copy-start(f32[128,128]{1,0:T(8,128)} %e_ref.1) | copy-start | bytes 196612
  39.5 20.9 %collective-permute-start = (bf16[8,256,256]{2,1,0:T(8,128)(2,1)S(1)}, bf16[8,256,256]{2,1,0:T(8,128)(2,1)S(1)}, u32[]{:S(2)}, u32[]{:S(2)}) collective-permute-start(bf16[8,256,256]{2,1,0:T(8,128)(2,1)S(1)} %bitcast.2), channel_id=1, source_target_pairs={{0,32},{32,0},{1,33},{33,1},{2,34},{34,2},{3,35},{35,3},{4,36},{36... | collective-permute-start | bytes 3145736 | tf_op jit(solution)/shard_map/ppermute | solution.py:117
  54.2 6.3 %collective-permute-start.2 = (bf16[16,16,128]{2,1,0:T(8,128)(2,1)S(1)}, bf16[16,16,128]{2,1,0:T(8,128)(2,1)S(1)}, u32[]{:S(2)}, u32[]{:S(2)}) collective-permute-start(bf16[16,16,128]{2,1,0:T(8,128)(2,1)S(1)} %slice.4), channel_id=1, source_target_pairs={{0,32},{32,0},{1,33},{33,1},{2,34},{34,2},{3,35},{35,3},{4,36},{36... | collective-permute-start | bytes 196616 | tf_op jit(solution)/shard_map/ppermute | solution.py:116

commit v3 on v2

--- a/solution.py
+++ b/solution.py
@@ -11,58 +11,75 @@
 LAG = ("x", "yl", "c")
 ROW = ("yh", "zh", "zl")
 TRADE = ("x", "yl", "zl")
-COPIES = ("yh", "zh")
 
 
-def swap_pairs(step):
+def spot(x, qy, c, yh, zh, qz):
+    lag = (x * 2 + (qy ^ yh // 2)) * 2 + c
+    return lag * 32 + (yh * 4 + zh) * 2 + (qz ^ zh // 2)
+
+
+def copy_groups():
+    return [
+        [spot(x, qy, c, yh, zh, qz) for yh in range(4) for zh in range(4)]
+        for x in range(4) for qy in range(2) for c in range(2) for qz in range(2)
+    ]
+
+
+def swap_pairs():
     pairs = []
-    for lag in range(16 - step):
+    for lag in range(16):
         for row in range(32):
-            x, yl, c = (lag + step) // 4, (lag + step) // 2 % 2, (lag + step) % 2
+            x, yl, c = lag // 4, lag // 2 % 2, lag % 2
             yh, zh, zl = row // 8, row // 2 % 4, row % 2
-            to_lag = (yh * 2 + zh % 2) * 2 + c
-            to_row = x * 8 + (zh // 2 * 2 + yl) * 2 + zl
-            pairs.append((lag * 32 + row, to_lag * 32 + to_row))
+            to_zh = zh // 2 * 2 + yl
+            pairs.append((lag * 32 + row, spot(yh, zh % 2, c, x, to_zh, zl ^ zh // 2)))
     return pairs
 
 
-def split_kernel(p_ref, o_ref, in_ref, out_ref, in_sem, out_sem):
+def split_kernel(flip_ref, p_ref, o_ref, in_ref, out_ref, at_ref, in_sem, out_sem, at_sem):
     parts = 4
+    fetch = pltpu.make_async_copy(flip_ref, at_ref, at_sem)
+    fetch.start()
     rows = B // parts
     loads = [pltpu.make_async_copy(p_ref.at[0, pl.ds(i * rows, rows)], in_ref.at[pl.ds(i * rows, rows)], in_sem.at[i]) for i in range(parts)]
     for load in loads:
         load.start()
+    fetch.wait()
+    flip = at_ref[0]
     stores = []
     for i in range(parts):
         loads[i].wait()
         here = slice(i * rows, (i + 1) * rows)
         for x in range(4):
-            for yl in range(2):
-                for zl in range(2):
+            for qy in range(2):
+                for qz in range(2):
+                    to = x * 4 + ((qy * 2 + qz) ^ flip)
                     for h in range(2):
-                        col = (x * 8 + h * 4 + yl * 2 + zl) * B
-                        out_ref[(x * 2 + yl) * 2 + zl, here, h * B:(h + 1) * B] = in_ref[here, col:col + B]
+                        col = (x * 8 + h * 4 + qy * 2 + (qz ^ h)) * B
+                        out_ref[to, here, h * B:(h + 1) * B] = in_ref[here, col:col + B]
         stores.append(pltpu.make_async_copy(out_ref.at[:, pl.ds(i * rows, rows)], o_ref.at[:, pl.ds(i * rows, rows)], out_sem.at[i]))
         stores[i].start()
     for store in stores:
         store.wait()
 
 
-def split_panels(panels):
+def split_panels(flip, panels):
     anywhere = pl.BlockSpec(memory_space=pl.ANY)
     return pl.pallas_call(
         split_kernel,
         out_shape=jax.ShapeDtypeStruct((16, B, 2 * B), jnp.bfloat16),
-        in_specs=[anywhere],
+        in_specs=[anywhere, anywhere],
         out_specs=anywhere,
         scratch_shapes=[
             pltpu.VMEM((B, 32 * B), jnp.bfloat16),
             pltpu.VMEM((16, B, 2 * B), jnp.bfloat16),
+            pltpu.SMEM((1,), jnp.int32),
             pltpu.SemaphoreType.DMA((4,)),
             pltpu.SemaphoreType.DMA((4,)),
+            pltpu.SemaphoreType.DMA,
         ],
         name="split",
-    )(panels)
+    )(flip, panels)
 
 
 def field_kernel(c_ref, own_ref, other_ref, x_ref, h_ref, e_ref, out_ref, kept_ref, s_ref):
@@ -110,12 +127,14 @@
 
 def body(currents, panels, excitation):
     everyone = LAG + ROW
-    own = lax.all_to_all(split_panels(panels), TRADE, 0, 0, tiled=True).reshape(8, 2 * B, 2 * B)
-    block = lax.ppermute(currents, everyone, swap_pairs(0))
-    x = lax.all_to_all(jnp.broadcast_to(block[None], (16,) + block.shape), COPIES, 0, 0, tiled=True)
+    core = lax.axis_index("c").astype(jnp.int32).reshape(1)
+    flip = (lax.axis_index("yh") // 2 * 2 + lax.axis_index("zh") // 2).astype(jnp.int32).reshape(1)
+    own = lax.all_to_all(split_panels(flip, panels), TRADE, 0, 0, tiled=True).reshape(8, 2 * B, 2 * B)
+    block = lax.ppermute(currents, everyone, swap_pairs())
+    copies = jnp.broadcast_to(block[None], (16,) + block.shape)
+    x = lax.all_to_all(copies, everyone, 0, 0, tiled=True, axis_index_groups=copy_groups())
     ends = lax.ppermute(x[:, B - HALO:], "c", [(0, 1), (1, 0)])
     other = lax.ppermute(own, "c", [(0, 1), (1, 0)])
-    core = lax.axis_index("c").astype(jnp.int32).reshape(1)
     part, kept = field_of(core, own, other, x, ends, excitation)
     got = lax.all_to_all(part.astype(jnp.float16), TRADE, 0, 0, tiled=True)
     return kept - jnp.sum(got.astype(jnp.float32), 0)

time: 83.7 us -> 80.2 us (0.958)
  blocking collectives: 19.6 us -> 13.7 us
  waiting for transfers between devices: 23.4 us -> 27 us
  starting transfers between devices: 34 us -> 32.7 us
    all_to_all x1, blocking collectives: 19.6 us -> 13.7 us  [body(): got = lax.all_to_all(part.astype(jnp.float16), TRADE, 0, 0, tiled=True)]
    all_to_all x2, waiting for transfers between devices: 22.5 us -> 26.2 us  [the longest x1 13.1 us: body(): lax.all_to_all(copies, everyone, 0, 0, tiled=True, axis_index_groups=copy...]
    ppermute x1, starting transfers between devices: 5.39 us -> 4.33 us  [body(): ends = lax.ppermute(x[:, B - HALO:], 'c', [(0, 1), (1, 0)])]
where the time goes in v3:
time: 80.2 us; the launch traced here: 79.7 us
  starting transfers between devices  32.7 us (41%)
  waiting for transfers between devices  27 us (34%)
  blocking collectives  13.7 us (17%)
  Pallas kernels  4.42 us (6%)
  local copies, waits for them, and re-layouts  0.91 us (1%)
  other arithmetic  0.82 us (1%)
    all_to_all x1, starting transfers between devices, body(): lax.all_to_all(copies, everyone, 0, 0, tiled=True, axis_index_groups=copy...  16.2 us
    all_to_all x1, blocking collectives, body(): got = lax.all_to_all(part.astype(jnp.float16), TRADE, 0, 0, tiled=True)  13.7 us
    all_to_all x1, waiting for transfers between devices, body(): lax.all_to_all(copies, everyone, 0, 0, tiled=True, axis_index_groups=copy...  13.1 us
    all_to_all x1, waiting for transfers between devices, body(): lax.all_to_all(split_panels(flip, panels), TRADE, 0, 0, tiled=True)  13.1 us
    all_to_all x1, starting transfers between devices, body(): lax.all_to_all(split_panels(flip, panels), TRADE, 0, 0, tiled=True)  7.79 us
    ppermute x1, starting transfers between devices, body(): ends = lax.ppermute(x[:, B - HALO:], 'c', [(0, 1), (1, 0)])  4.33 us
    ppermute x1, starting transfers between devices, body(): other = lax.ppermute(own, 'c', [(0, 1), (1, 0)])  3.7 us
    pallas_call x1, Pallas kernels, field_of(): pl.pallas_call(field_kernel, out_shape=(jax.ShapeDtypeStruct((16, B, B),...  2.37 us
  transfers between devices with their start and end apart: 5, of which 3 were waited for; matrix products, arithmetic and copies ran while one was open for 0% of the time, Pallas kernels for 0%

profile of v3, /device:TPU:1, one launch (start us, length us, event | category | flops | bytes accessed | tf_op | source)
XLA Modules:
  0.0 79.7 jit_solution(3303223179693210387)
XLA Ops:
  0.0 2.0 %split.1 = bf16[16,128,256]{2,1,0:T(8,128)(2,1)} custom-call(s32[1]{0:T(128)} %bitcast.1.flip_ref, bf16[1,128,4096]{2,1,0:T(8,128)(2,1)} %p_ref.1), custom_call_target="tpu_custom_call" | custom-call | tf_op jit(solution)/shard_map/split/pallas_call | solution.py:68
  2.1 0.0 copy-start.1
  2.1 7.8 %all-to-all-start = ((bf16[16,128,256]{2,1,0:T(8,128)(2,1)}), bf16[16,128,256]{2,1,0:T(8,128)(2,1)S(1)}, u32[]{:S(2)}, u32[]{:S(2)}) async-start(bf16[16,128,256]{2,1,0:T(8,128)(2,1)} %split.1), calls=%async_computation | async-start | bytes 2097152 | tf_op jit(solution)/shard_map/all_to_all | solution.py:132
  9.9 0.0 copy-done.1
  9.9 0.7 collective-permute-start.1
  10.5 0.0 collective-permute-done.1
  10.6 13.1 %all-to-all-done = bf16[16,128,256]{2,1,0:T(8,128)(2,1)S(1)} async-done(((bf16[16,128,256]{2,1,0:T(8,128)(2,1)}), bf16[16,128,256]{2,1,0:T(8,128)(2,1)S(1)}, u32[]{:S(2)}, u32[]{:S(2)}) %all-to-all-start) | async-done | bytes 1048608 | tf_op jit(solution)/shard_map/all_to_all | solution.py:132
  23.6 0.9 %broadcast_in_dim.2 = bf16[16,128,128]{2,1,0:T(8,128)(2,1)} broadcast(bf16[128,128]{1,0:T(8,128)(2,1)S(1)} %collective-permute-done.1), dimensions={1,2} | broadcast | bytes 557056 | tf_op jit(solution)/shard_map/broadcast_in_dim | solution.py:134
  24.5 16.2 %all-to-all-start.1 = ((bf16[16,128,128]{2,1,0:T(8,128)(2,1)}), bf16[16,128,128]{2,1,0:T(8,128)(2,1)S(1)}, u32[]{:S(2)}, u32[]{:S(2)}) async-start(bf16[16,128,128]{2,1,0:T(8,128)(2,1)} %broadcast_in_dim.2), calls=%async_computation.1 | async-start | bytes 1048576 | tf_op jit(solution)/shard_map/all_to_all | solution.py:135
  40.7 0.0 copy-start
  40.7 3.7 %collective-permute-start = (bf16[8,256,256]{2,1,0:T(8,128)(2,1)S(1)}, bf16[8,256,256]{2,1,0:T(8,128)(2,1)S(1)}, u32[]{:S(2)}, u32[]{:S(2)}) collective-permute-start(bf16[8,256,256]{2,1,0:T(8,128)(2,1)S(1)} %bitcast.3), channel_id=1, source_target_pairs={{0,32},{32,0},{1,33},{33,1},{2,34},{34,2},{3,35},{35,3},{4,36},{36... | collective-permute-start | bytes 3145736 | tf_op jit(solution)/shard_map/ppermute | solution.py:137
  44.4 13.1 %all-to-all-done.1.x_ref = bf16[16,128,128]{2,1,0:T(8,128)(2,1)S(1)} async-done(((bf16[16,128,128]{2,1,0:T(8,128)(2,1)}), bf16[16,128,128]{2,1,0:T(8,128)(2,1)S(1)}, u32[]{:S(2)}, u32[]{:S(2)}) %all-to-all-start.1) | async-done | bytes 524320 | tf_op jit(solution)/shard_map/all_to_all | solution.py:135
  57.6 4.3 %collective-permute-start.2 = (bf16[16,16,128]{2,1,0:T(8,128)(2,1)S(1)}, bf16[16,16,128]{2,1,0:T(8,128)(2,1)S(1)}, u32[]{:S(2)}, u32[]{:S(2)}) collective-permute-start(bf16[16,16,128]{2,1,0:T(8,128)(2,1)S(1)} %slice.4), channel_id=1, source_target_pairs={{0,32},{32,0},{1,33},{33,1},{2,34},{34,2},{3,35},{35,3},{4,36},{36... | collective-permute-start | bytes 196616 | tf_op jit(solution)/shard_map/ppermute | solution.py:136
  61.9 0.9 %collective-permute-done.2.h_ref = bf16[16,16,128]{2,1,0:T(8,128)(2,1)S(1)} collective-permute-done((bf16[16,16,128]{2,1,0:T(8,128)(2,1)S(1)}, bf16[16,16,128]{2,1,0:T(8,128)(2,1)S(1)}, u32[]{:S(2)}, u32[]{:S(2)}) %collective-permute-start.2) | collective-permute-done | bytes 65568 | tf_op jit(solution)/shard_map/ppermute | solution.py:136
  62.8 0.0 collective-permute-done.other_ref
  62.8 0.0 copy-done
  62.8 2.4 %field.1 = (f32[16,128,128]{2,1,0:T(8,128)S(1)}, f32[128,128]{1,0:T(8,128)S(1)}) custom-call(s32[1]{0:T(128)} %bitcast.c_ref, bf16[8,256,256]{2,1,0:T(8,128)(2,1)S(1)} %bitcast.4, bf16[8,256,256]{2,1,0:T(8,128)(2,1)S(1)} %collective-permute-done.other_ref, bf16[16,128,128]{2,1,0:T(8,128)(2,1)S(1)} %all-to-all-done.1.x_ref, ...), custom_call_target="tpu_custom_call" | custom-call | tf_op jit(solution)/shard_map/field/pallas_call | solution.py:117
  65.2 0.1 convert_element_type.6
  65.3 13.7 %all_to_all.15 = f16[16,128,128]{2,1,0:T(8,128)(2,1)S(1)} all-to-all(f16[16,128,128]{2,1,0:T(8,128)(2,1)S(1)} %convert_element_type.6), channel_id=1, replica_groups=mesh['x'=4,'yl'=2,'c'=2,'yh'=4,'zh'=4,'zl'=2] {'x','yl','zl'}, dimensions={0} | all-to-all | bytes 1048576 | tf_op jit(solution)/shard_map/all_to_all | solution.py:139
  79.0 0.1 convert_reduce_fusion
  79.1 0.6 sub.12
  (1 shorter events, 0.0 us)
Async XLA Ops:
  2.1 7.8 %copy-start.1 = (bf16[128,128]{1,0:T(8,128)(2,1)S(1)}, bf16[128,128]{1,0:T(8,128)(2,1)}, u32[]{:S(2)}) copy-start(bf16[128,128]{1,0:T(8,128)(2,1)} %param.3) | copy-start | bytes 98308
  2.1 21.6 %all-to-all-start = ((bf16[16,128,256]{2,1,0:T(8,128)(2,1)}), bf16[16,128,256]{2,1,0:T(8,128)(2,1)S(1)}, u32[]{:S(2)}, u32[]{:S(2)}) async-start(bf16[16,128,256]{2,1,0:T(8,128)(2,1)} %split.1), calls=%async_computation | async-start | bytes 2097152 | tf_op jit(solution)/shard_map/all_to_all | solution.py:132
  9.9 0.7 collective-permute-start.1
  24.5 33.0 %all-to-all-start.1 = ((bf16[16,128,128]{2,1,0:T(8,128)(2,1)}), bf16[16,128,128]{2,1,0:T(8,128)(2,1)S(1)}, u32[]{:S(2)}, u32[]{:S(2)}) async-start(bf16[16,128,128]{2,1,0:T(8,128)(2,1)} %broadcast_in_dim.2), calls=%async_computation.1 | async-start | bytes 1048576 | tf_op jit(solution)/shard_map/all_to_all | solution.py:135
  40.7 22.0 %copy-start = (f32[128,128]{1,0:T(8,128)S(1)}, f32[128,128]{1,0:T(8,128)}, u32[]{:S(2)}) copy-start(f32[128,128]{1,0:T(8,128)} %e_ref.1) | copy-start | bytes 196612
  40.7 22.0 %collective-permute-start = (bf16[8,256,256]{2,1,0:T(8,128)(2,1)S(1)}, bf16[8,256,256]{2,1,0:T(8,128)(2,1)S(1)}, u32[]{:S(2)}, u32[]{:S(2)}) collective-permute-start(bf16[8,256,256]{2,1,0:T(8,128)(2,1)S(1)} %bitcast.3), channel_id=1, source_target_pairs={{0,32},{32,0},{1,33},{33,1},{2,34},{34,2},{3,35},{35,3},{4,36},{36... | collective-permute-start | bytes 3145736 | tf_op jit(solution)/shard_map/ppermute | solution.py:137
  57.6 5.2 %collective-permute-start.2 = (bf16[16,16,128]{2,1,0:T(8,128)(2,1)S(1)}, bf16[16,16,128]{2,1,0:T(8,128)(2,1)S(1)}, u32[]{:S(2)}, u32[]{:S(2)}) collective-permute-start(bf16[16,16,128]{2,1,0:T(8,128)(2,1)S(1)} %slice.4), channel_id=1, source_target_pairs={{0,32},{32,0},{1,33},{33,1},{2,34},{34,2},{3,35},{35,3},{4,36},{36... | collective-permute-start | bytes 196616 | tf_op jit(solution)/shard_map/ppermute | solution.py:136

commit v4 on v3

--- a/solution.py
+++ b/solution.py
@@ -11,29 +11,48 @@
 LAG = ("x", "yl", "c")
 ROW = ("yh", "zh", "zl")
 TRADE = ("x", "yl", "zl")
+SETS = (
+    (0, 29), (4, 25), (8, 21), (9, 20),
+    (1, 30), (5, 26), (10, 23), (11, 22),
+    (2, 31), (6, 27), (13, 16), (12, 17),
+    (3, 24), (7, 28), (15, 18), (14, 19),
+)
+HOLDS = (
+    (8, 5, 1, 7, 0, 4, 3, 12, 9, 13, 10, 15, 14, 2, 11, 6),
+    (10, 7, 14, 1, 2, 6, 3, 5, 11, 4, 8, 13, 12, 0, 9, 15),
+    (1, 12, 0, 8, 4, 7, 3, 5, 9, 13, 11, 6, 10, 14, 2, 15),
+    (3, 12, 4, 5, 0, 8, 1, 7, 2, 15, 6, 13, 10, 14, 11, 9),
+    (13, 4, 9, 7, 12, 5, 1, 0, 10, 2, 8, 6, 11, 3, 15, 14),
+    (15, 6, 11, 5, 14, 7, 3, 2, 8, 0, 10, 4, 9, 1, 13, 12),
+    (1, 13, 2, 6, 0, 4, 5, 9, 10, 8, 3, 14, 7, 12, 11, 15),
+    (1, 4, 0, 13, 2, 6, 5, 9, 10, 14, 3, 12, 8, 11, 7, 15),
+    (1, 5, 0, 13, 2, 6, 9, 4, 11, 15, 8, 12, 10, 7, 3, 14),
+    (3, 7, 2, 15, 0, 4, 11, 6, 9, 13, 10, 14, 8, 5, 1, 12),
+    (2, 6, 10, 7, 1, 5, 3, 14, 8, 12, 9, 15, 0, 13, 4, 11),
+    (2, 6, 1, 5, 3, 14, 10, 7, 8, 12, 9, 4, 0, 15, 11, 13),
+    (2, 6, 1, 5, 0, 13, 14, 4, 11, 3, 8, 12, 9, 15, 10, 7),
+    (0, 4, 3, 7, 2, 15, 12, 6, 9, 1, 10, 14, 11, 13, 8, 5),
+    (0, 4, 3, 7, 11, 6, 2, 15, 8, 12, 9, 13, 1, 5, 10, 14),
+    (3, 6, 7, 11, 2, 4, 0, 15, 8, 14, 9, 13, 5, 10, 1, 12),
+)
 
 
-def spot(x, qy, c, yh, zh, qz):
+def holder(s, c, piece):
+    x, qy, qz = s // 4, s // 2 % 2, s % 2
+    yh, zh = HOLDS[s][piece] // 4, HOLDS[s][piece] % 4
     lag = (x * 2 + (qy ^ yh // 2)) * 2 + c
     return lag * 32 + (yh * 4 + zh) * 2 + (qz ^ zh // 2)
 
 
 def copy_groups():
-    return [
-        [spot(x, qy, c, yh, zh, qz) for yh in range(4) for zh in range(4)]
-        for x in range(4) for qy in range(2) for c in range(2) for qz in range(2)
-    ]
+    return [[holder(s, c, piece) for piece in range(16)] for s in range(16) for c in range(2)]
 
 
 def swap_pairs():
-    pairs = []
-    for lag in range(16):
-        for row in range(32):
-            x, yl, c = lag // 4, lag // 2 % 2, lag % 2
-            yh, zh, zl = row // 8, row // 2 % 4, row % 2
-            to_zh = zh // 2 * 2 + yl
-            pairs.append((lag * 32 + row, spot(yh, zh % 2, c, x, to_zh, zl ^ zh // 2)))
-    return pairs
+    return [
+        ((m * 2 + c) * 32 + SETS[s][h], holder(s, c, h * 8 + m))
+        for s in range(16) for c in range(2) for h in range(2) for m in range(8)
+    ]
 
 
 def split_kernel(flip_ref, p_ref, o_ref, in_ref, out_ref, at_ref, in_sem, out_sem, at_sem):
@@ -55,7 +74,7 @@
                 for qz in range(2):
                     to = x * 4 + ((qy * 2 + qz) ^ flip)
                     for h in range(2):
-                        col = (x * 8 + h * 4 + qy * 2 + (qz ^ h)) * B
+                        col = SETS[x * 4 + qy * 2 + qz][h] * B
                         out_ref[to, here, h * B:(h + 1) * B] = in_ref[here, col:col + B]
         stores.append(pltpu.make_async_copy(out_ref.at[:, pl.ds(i * rows, rows)], o_ref.at[:, pl.ds(i * rows, rows)], out_sem.at[i]))
         stores[i].start()
@@ -87,7 +106,7 @@
     kept_ref[...] = e_ref[...]
 
     def place(m, h):
-        return (m // 2) * 4 + h * 2 + m % 2
+        return h * 8 + m
 
     def run(c):
         for m in range(8):

time: 80.2 us -> 77.9 us (0.971)
  waiting for transfers between devices: 27 us -> 15.9 us
  starting transfers between devices: 32.7 us -> 41.6 us
    all_to_all x1, waiting for transfers between devices: 13.1 us -> 0.4 us  [body(): lax.all_to_all(split_panels(flip, panels), TRADE, 0, 0, tiled=True)]
    ppermute x1, starting transfers between devices: 0.66 us -> 6.73 us  [body(): block = lax.ppermute(currents, everyone, swap_pairs())]
    ppermute x1, waiting for transfers between devices: 0.01 us -> 5.91 us  [body(): block = lax.ppermute(currents, everyone, swap_pairs())]
    all_to_all x1, waiting for transfers between devices: 13.1 us -> 8.72 us  [body(): lax.all_to_all(copies, everyone, 0, 0, tiled=True, axis_index_groups=copy...]
    ppermute x1, starting transfers between devices: 4.33 us -> 5.84 us  [body(): ends = lax.ppermute(x[:, B - HALO:], 'c', [(0, 1), (1, 0)])]
    all_to_all x1, starting transfers between devices: 16.2 us -> 17.1 us  [body(): lax.all_to_all(copies, everyone, 0, 0, tiled=True, axis_index_groups=copy...]
  transfers between devices with their start and end apart: 5 -> 5, of which waited for: 3 -> 4; matrix products, arithmetic and copies ran while one was open for 0% -> 0% of each run, Pallas kernels for 0% -> 0%
where the time goes in v4:
time: 77.9 us; the launch traced here: 77.4 us
  starting transfers between devices  41.6 us (53%)
  waiting for transfers between devices  15.9 us (20%)
  blocking collectives  13.6 us (17%)
  Pallas kernels  4.41 us (6%)
  local copies, waits for them, and re-layouts  0.91 us (1%)
  other arithmetic  0.82 us (1%)
    all_to_all x1, starting transfers between devices, body(): lax.all_to_all(copies, everyone, 0, 0, tiled=True, axis_index_groups=copy...  17.1 us
    all_to_all x1, blocking collectives, body(): got = lax.all_to_all(part.astype(jnp.float16), TRADE, 0, 0, tiled=True)  13.6 us
    all_to_all x1, waiting for transfers between devices, body(): lax.all_to_all(copies, everyone, 0, 0, tiled=True, axis_index_groups=copy...  8.72 us
    all_to_all x1, starting transfers between devices, body(): lax.all_to_all(split_panels(flip, panels), TRADE, 0, 0, tiled=True)  7.79 us
    ppermute x1, starting transfers between devices, body(): block = lax.ppermute(currents, everyone, swap_pairs())  6.73 us
    ppermute x1, waiting for transfers between devices, body(): block = lax.ppermute(currents, everyone, swap_pairs())  5.91 us
    ppermute x1, starting transfers between devices, body(): ends = lax.ppermute(x[:, B - HALO:], 'c', [(0, 1), (1, 0)])  5.84 us
    ppermute x1, starting transfers between devices, body(): other = lax.ppermute(own, 'c', [(0, 1), (1, 0)])  4.17 us
  transfers between devices with their start and end apart: 5, of which 4 were waited for; matrix products, arithmetic and copies ran while one was open for 0% of the time, Pallas kernels for 0%

profile of v4, /device:TPU:1, one launch (start us, length us, event | category | flops | bytes accessed | tf_op | source)
XLA Modules:
  0.0 77.4 jit_solution(6808016433499913019)
XLA Ops:
  0.0 2.0 %split.1 = bf16[16,128,256]{2,1,0:T(8,128)(2,1)} custom-call(s32[1]{0:T(128)} %bitcast.1.flip_ref, bf16[1,128,4096]{2,1,0:T(8,128)(2,1)} %p_ref.1), custom_call_target="tpu_custom_call" | custom-call | tf_op jit(solution)/shard_map/split/pallas_call | solution.py:87
  2.1 0.0 copy-start.1
  2.1 7.8 %all-to-all-start = ((bf16[16,128,256]{2,1,0:T(8,128)(2,1)}), bf16[16,128,256]{2,1,0:T(8,128)(2,1)S(1)}, u32[]{:S(2)}, u32[]{:S(2)}) async-start(bf16[16,128,256]{2,1,0:T(8,128)(2,1)} %split.1), calls=%async_computation | async-start | bytes 2097152 | tf_op jit(solution)/shard_map/all_to_all | solution.py:151
  9.9 0.0 copy-done.1
  9.9 6.7 %collective-permute-start.1 = (bf16[128,128]{1,0:T(8,128)(2,1)S(1)}, bf16[128,128]{1,0:T(8,128)(2,1)S(1)}, u32[]{:S(2)}, u32[]{:S(2)}) collective-permute-start(bf16[128,128]{1,0:T(8,128)(2,1)S(1)} %copy-done.1), channel_id=1, source_target_pairs={{0,80},{64,10},{128,2},{192,15},{256,0},{320,8},{384,7},{448,88},{... | collective-permute-start | bytes 98312 | tf_op jit(solution)/shard_map/ppermute | solution.py:152
  16.6 5.9 %collective-permute-done.1 = bf16[128,128]{1,0:T(8,128)(2,1)S(1)} collective-permute-done((bf16[128,128]{1,0:T(8,128)(2,1)S(1)}, bf16[128,128]{1,0:T(8,128)(2,1)S(1)}, u32[]{:S(2)}, u32[]{:S(2)}) %collective-permute-start.1) | collective-permute-done | bytes 32800 | tf_op jit(solution)/shard_map/ppermute | solution.py:152
  22.5 0.4 all-to-all-done
  22.9 0.9 %broadcast_in_dim.2 = bf16[16,128,128]{2,1,0:T(8,128)(2,1)} broadcast(bf16[128,128]{1,0:T(8,128)(2,1)S(1)} %collective-permute-done.1), dimensions={1,2} | broadcast | bytes 557056 | tf_op jit(solution)/shard_map/broadcast_in_dim | solution.py:153
  23.8 17.1 %all-to-all-start.1 = ((bf16[16,128,128]{2,1,0:T(8,128)(2,1)}), bf16[16,128,128]{2,1,0:T(8,128)(2,1)S(1)}, u32[]{:S(2)}, u32[]{:S(2)}) async-start(bf16[16,128,128]{2,1,0:T(8,128)(2,1)} %broadcast_in_dim.2), calls=%async_computation.1 | async-start | bytes 1048576 | tf_op jit(solution)/shard_map/all_to_all | solution.py:154
  40.9 0.0 copy-start
  40.9 4.2 %collective-permute-start = (bf16[8,256,256]{2,1,0:T(8,128)(2,1)S(1)}, bf16[8,256,256]{2,1,0:T(8,128)(2,1)S(1)}, u32[]{:S(2)}, u32[]{:S(2)}) collective-permute-start(bf16[8,256,256]{2,1,0:T(8,128)(2,1)S(1)} %bitcast.3), channel_id=1, source_target_pairs={{0,32},{32,0},{1,33},{33,1},{2,34},{34,2},{3,35},{35,3},{4,36},{36... | collective-permute-start | bytes 3145736 | tf_op jit(solution)/shard_map/ppermute | solution.py:156
  45.1 8.7 %all-to-all-done.1.x_ref = bf16[16,128,128]{2,1,0:T(8,128)(2,1)S(1)} async-done(((bf16[16,128,128]{2,1,0:T(8,128)(2,1)}), bf16[16,128,128]{2,1,0:T(8,128)(2,1)S(1)}, u32[]{:S(2)}, u32[]{:S(2)}) %all-to-all-start.1) | async-done | bytes 524320 | tf_op jit(solution)/shard_map/all_to_all | solution.py:154
  53.8 5.8 %collective-permute-start.2 = (bf16[16,16,128]{2,1,0:T(8,128)(2,1)S(1)}, bf16[16,16,128]{2,1,0:T(8,128)(2,1)S(1)}, u32[]{:S(2)}, u32[]{:S(2)}) collective-permute-start(bf16[16,16,128]{2,1,0:T(8,128)(2,1)S(1)} %slice.4), channel_id=1, source_target_pairs={{0,32},{32,0},{1,33},{33,1},{2,34},{34,2},{3,35},{35,3},{4,36},{36... | collective-permute-start | bytes 196616 | tf_op jit(solution)/shard_map/ppermute | solution.py:155
  59.7 0.9 %collective-permute-done.2.h_ref = bf16[16,16,128]{2,1,0:T(8,128)(2,1)S(1)} collective-permute-done((bf16[16,16,128]{2,1,0:T(8,128)(2,1)S(1)}, bf16[16,16,128]{2,1,0:T(8,128)(2,1)S(1)}, u32[]{:S(2)}, u32[]{:S(2)}) %collective-permute-start.2) | collective-permute-done | bytes 65568 | tf_op jit(solution)/shard_map/ppermute | solution.py:155
  60.6 0.0 collective-permute-done.other_ref
  60.6 0.0 copy-done
  60.6 2.4 %field.1 = (f32[16,128,128]{2,1,0:T(8,128)S(1)}, f32[128,128]{1,0:T(8,128)S(1)}) custom-call(s32[1]{0:T(128)} %bitcast.c_ref, bf16[8,256,256]{2,1,0:T(8,128)(2,1)S(1)} %bitcast.4, bf16[8,256,256]{2,1,0:T(8,128)(2,1)S(1)} %collective-permute-done.other_ref, bf16[16,128,128]{2,1,0:T(8,128)(2,1)S(1)} %all-to-all-done.1.x_ref, ...), custom_call_target="tpu_custom_call" | custom-call | tf_op jit(solution)/shard_map/field/pallas_call | solution.py:136
  62.9 0.1 convert_element_type.6
  63.1 13.6 %all_to_all.15 = f16[16,128,128]{2,1,0:T(8,128)(2,1)S(1)} all-to-all(f16[16,128,128]{2,1,0:T(8,128)(2,1)S(1)} %convert_element_type.6), channel_id=1, replica_groups=mesh['x'=4,'yl'=2,'c'=2,'yh'=4,'zh'=4,'zl'=2] {'x','yl','zl'}, dimensions={0} | all-to-all | bytes 1048576 | tf_op jit(solution)/shard_map/all_to_all | solution.py:158
  76.7 0.1 convert_reduce_fusion
  76.8 0.6 sub.12
  (1 shorter events, 0.0 us)
Async XLA Ops:
  2.1 7.8 %copy-start.1 = (bf16[128,128]{1,0:T(8,128)(2,1)S(1)}, bf16[128,128]{1,0:T(8,128)(2,1)}, u32[]{:S(2)}) copy-start(bf16[128,128]{1,0:T(8,128)(2,1)} %param.3) | copy-start | bytes 98308
  2.1 20.9 %all-to-all-start = ((bf16[16,128,256]{2,1,0:T(8,128)(2,1)}), bf16[16,128,256]{2,1,0:T(8,128)(2,1)S(1)}, u32[]{:S(2)}, u32[]{:S(2)}) async-start(bf16[16,128,256]{2,1,0:T(8,128)(2,1)} %split.1), calls=%async_computation | async-start | bytes 2097152 | tf_op jit(solution)/shard_map/all_to_all | solution.py:151
  9.9 12.6 %collective-permute-start.1 = (bf16[128,128]{1,0:T(8,128)(2,1)S(1)}, bf16[128,128]{1,0:T(8,128)(2,1)S(1)}, u32[]{:S(2)}, u32[]{:S(2)}) collective-permute-start(bf16[128,128]{1,0:T(8,128)(2,1)S(1)} %copy-done.1), channel_id=1, source_target_pairs={{0,80},{64,10},{128,2},{192,15},{256,0},{320,8},{384,7},{448,88},{... | collective-permute-start | bytes 98312 | tf_op jit(solution)/shard_map/ppermute | solution.py:152
  23.8 30.0 %all-to-all-start.1 = ((bf16[16,128,128]{2,1,0:T(8,128)(2,1)}), bf16[16,128,128]{2,1,0:T(8,128)(2,1)S(1)}, u32[]{:S(2)}, u32[]{:S(2)}) async-start(bf16[16,128,128]{2,1,0:T(8,128)(2,1)} %broadcast_in_dim.2), calls=%async_computation.1 | async-start | bytes 1048576 | tf_op jit(solution)/shard_map/all_to_all | solution.py:154
  40.9 19.6 %copy-start = (f32[128,128]{1,0:T(8,128)S(1)}, f32[128,128]{1,0:T(8,128)}, u32[]{:S(2)}) copy-start(f32[128,128]{1,0:T(8,128)} %e_ref.1) | copy-start | bytes 196612
  40.9 19.6 %collective-permute-start = (bf16[8,256,256]{2,1,0:T(8,128)(2,1)S(1)}, bf16[8,256,256]{2,1,0:T(8,128)(2,1)S(1)}, u32[]{:S(2)}, u32[]{:S(2)}) collective-permute-start(bf16[8,256,256]{2,1,0:T(8,128)(2,1)S(1)} %bitcast.3), channel_id=1, source_target_pairs={{0,32},{32,0},{1,33},{33,1},{2,34},{34,2},{3,35},{35,3},{4,36},{36... | collective-permute-start | bytes 3145736 | tf_op jit(solution)/shard_map/ppermute | solution.py:156
  53.8 6.7 %collective-permute-start.2 = (bf16[16,16,128]{2,1,0:T(8,128)(2,1)S(1)}, bf16[16,16,128]{2,1,0:T(8,128)(2,1)S(1)}, u32[]{:S(2)}, u32[]{:S(2)}) collective-permute-start(bf16[16,16,128]{2,1,0:T(8,128)(2,1)S(1)} %slice.4), channel_id=1, source_target_pairs={{0,32},{32,0},{1,33},{33,1},{2,34},{34,2},{3,35},{35,3},{4,36},{36... | collective-permute-start | bytes 196616 | tf_op jit(solution)/shard_map/ppermute | solution.py:155

commit v5 on v4

--- a/solution.py
+++ b/solution.py
@@ -37,6 +37,9 @@
 )
 
 
+ORDER = (11, 15, 10, 14, 7, 3, 6, 2, 9, 13, 5, 8, 1, 12, 4, 0)
+
+
 def holder(s, c, piece):
     x, qy, qz = s // 4, s // 2 % 2, s % 2
     yh, zh = HOLDS[s][piece] // 4, HOLDS[s][piece] % 4
@@ -45,7 +48,12 @@
 
 
 def copy_groups():
-    return [[holder(s, c, piece) for piece in range(16)] for s in range(16) for c in range(2)]
+    return [[holder(s, c, HOLDS[s].index(spot)) for spot in ORDER] for s in range(16) for c in range(2)]
+
+
+def packed(places):
+    word = sum(ORDER.index(place) << 4 * i for i, place in enumerate(places))
+    return word - (1 << 32) if word >= 1 << 31 else word
 
 
 def swap_pairs():
@@ -55,16 +63,13 @@
     ]
 
 
-def split_kernel(flip_ref, p_ref, o_ref, in_ref, out_ref, at_ref, in_sem, out_sem, at_sem):
+def split_kernel(p_ref, o_ref, in_ref, out_ref, in_sem, out_sem):
     parts = 4
-    fetch = pltpu.make_async_copy(flip_ref, at_ref, at_sem)
-    fetch.start()
     rows = B // parts
     loads = [pltpu.make_async_copy(p_ref.at[0, pl.ds(i * rows, rows)], in_ref.at[pl.ds(i * rows, rows)], in_sem.at[i]) for i in range(parts)]
     for load in loads:
         load.start()
-    fetch.wait()
-    flip = at_ref[0]
+    flip = lax.axis_index("yh") // 2 * 2 + lax.axis_index("zh") // 2
     stores = []
     for i in range(parts):
         loads[i].wait()
@@ -82,31 +87,38 @@
         store.wait()
 
 
-def split_panels(flip, panels):
+def split_panels(panels):
     anywhere = pl.BlockSpec(memory_space=pl.ANY)
     return pl.pallas_call(
         split_kernel,
         out_shape=jax.ShapeDtypeStruct((16, B, 2 * B), jnp.bfloat16),
-        in_specs=[anywhere, anywhere],
+        in_specs=[anywhere],
         out_specs=anywhere,
         scratch_shapes=[
             pltpu.VMEM((B, 32 * B), jnp.bfloat16),
             pltpu.VMEM((16, B, 2 * B), jnp.bfloat16),
-            pltpu.SMEM((1,), jnp.int32),
             pltpu.SemaphoreType.DMA((4,)),
             pltpu.SemaphoreType.DMA((4,)),
-            pltpu.SemaphoreType.DMA,
         ],
         name="split",
-    )(flip, panels)
+    )(panels)
 
 
-def field_kernel(c_ref, own_ref, other_ref, x_ref, h_ref, e_ref, out_ref, kept_ref, s_ref):
-    core = c_ref[0]
+def field_kernel(own_ref, other_ref, x_ref, h_ref, e_ref, out_ref, kept_ref, s_ref):
+    core = lax.axis_index("c")
     kept_ref[...] = e_ref[...]
+    qy = lax.axis_index("yl") ^ lax.axis_index("yh") // 2
+    qz = lax.axis_index("zl") ^ lax.axis_index("zh") // 2
+    mine = lax.axis_index("x") * 4 + qy * 2 + qz
+    words = []
+    for h in range(2):
+        word = jnp.int32(0)
+        for s in range(16):
+            word = jnp.where(mine == s, jnp.int32(packed(HOLDS[s][h * 8:h * 8 + 8])), word)
+        words.append(word)
 
     def place(m, h):
-        return h * 8 + m
+        return (words[h] >> 4 * m) & 15
 
     def run(c):
         for m in range(8):
@@ -131,30 +143,28 @@
     pl.when(core == 1)(lambda: run(1))
 
 
-def field_of(core, own, other, x, ends, excitation):
+def field_of(own, other, x, ends, excitation):
     vmem = pl.BlockSpec(memory_space=pltpu.VMEM)
     return pl.pallas_call(
         field_kernel,
         out_shape=(jax.ShapeDtypeStruct((16, B, B), jnp.float32), jax.ShapeDtypeStruct((B, B), jnp.float32)),
-        in_specs=[pl.BlockSpec(memory_space=pltpu.SMEM)] + [vmem] * 5,
+        in_specs=[vmem] * 5,
         out_specs=(vmem, vmem),
         scratch_shapes=[pltpu.VMEM((8, HALO + B, 2 * B), jnp.float32)],
         compiler_params=pltpu.CompilerParams(vmem_limit_bytes=48 * 1024 * 1024),
         name="field",
-    )(core, own, other, x, ends, excitation)
+    )(own, other, x, ends, excitation)
 
 
 def body(currents, panels, excitation):
     everyone = LAG + ROW
-    core = lax.axis_index("c").astype(jnp.int32).reshape(1)
-    flip = (lax.axis_index("yh") // 2 * 2 + lax.axis_index("zh") // 2).astype(jnp.int32).reshape(1)
-    own = lax.all_to_all(split_panels(flip, panels), TRADE, 0, 0, tiled=True).reshape(8, 2 * B, 2 * B)
+    own = lax.all_to_all(split_panels(panels), TRADE, 0, 0, tiled=True).reshape(8, 2 * B, 2 * B)
     block = lax.ppermute(currents, everyone, swap_pairs())
     copies = jnp.broadcast_to(block[None], (16,) + block.shape)
     x = lax.all_to_all(copies, everyone, 0, 0, tiled=True, axis_index_groups=copy_groups())
     ends = lax.ppermute(x[:, B - HALO:], "c", [(0, 1), (1, 0)])
     other = lax.ppermute(own, "c", [(0, 1), (1, 0)])
-    part, kept = field_of(core, own, other, x, ends, excitation)
+    part, kept = field_of(own, other, x, ends, excitation)
     got = lax.all_to_all(part.astype(jnp.float16), TRADE, 0, 0, tiled=True)
     return kept - jnp.sum(got.astype(jnp.float32), 0)
 

time: 77.9 us -> 75.5 us (0.969)
  starting transfers between devices: 41.6 us -> 39.3 us
  blocking collectives: 13.6 us -> 12.2 us
  waiting for transfers between devices: 15.9 us -> 17.3 us
    ppermute x1, starting transfers between devices: 5.84 us -> 3.38 us  [body(): ends = lax.ppermute(x[:, B - HALO:], 'c', [(0, 1), (1, 0)])]
    all_to_all x1, blocking collectives: 13.6 us -> 12.2 us  [body(): got = lax.all_to_all(part.astype(jnp.float16), TRADE, 0, 0, tiled=True)]
    all_to_all x1, waiting for transfers between devices: 8.72 us -> 10.1 us  [body(): lax.all_to_all(copies, everyone, 0, 0, tiled=True, axis_index_groups=copy...]
    all_to_all x1, starting transfers between devices: 17.1 us -> 18.5 us  [body(): lax.all_to_all(copies, everyone, 0, 0, tiled=True, axis_index_groups=copy...]
    ppermute x1, starting transfers between devices: 4.17 us -> 2.93 us  [body(): other = lax.ppermute(own, 'c', [(0, 1), (1, 0)])]
where the time goes in v5:
time: 75.5 us; the launch traced here: 75 us
  starting transfers between devices  39.3 us (52%)
  waiting for transfers between devices  17.3 us (23%)
  blocking collectives  12.2 us (16%)
  Pallas kernels  4.44 us (6%)
  local copies, waits for them, and re-layouts  0.91 us (1%)
  other arithmetic  0.82 us (1%)
    all_to_all x1, starting transfers between devices, body(): lax.all_to_all(copies, everyone, 0, 0, tiled=True, axis_index_groups=copy...  18.5 us
    all_to_all x1, blocking collectives, body(): got = lax.all_to_all(part.astype(jnp.float16), TRADE, 0, 0, tiled=True)  12.2 us
    all_to_all x1, waiting for transfers between devices, body(): lax.all_to_all(copies, everyone, 0, 0, tiled=True, axis_index_groups=copy...  10.1 us
    all_to_all x1, starting transfers between devices, body(): lax.all_to_all(split_panels(panels), TRADE, 0, 0, tiled=True)  7.79 us
    ppermute x1, starting transfers between devices, body(): block = lax.ppermute(currents, everyone, swap_pairs())  6.73 us
    ppermute x1, waiting for transfers between devices, body(): block = lax.ppermute(currents, everyone, swap_pairs())  5.91 us
    ppermute x1, starting transfers between devices, body(): ends = lax.ppermute(x[:, B - HALO:], 'c', [(0, 1), (1, 0)])  3.38 us
    ppermute x1, starting transfers between devices, body(): other = lax.ppermute(own, 'c', [(0, 1), (1, 0)])  2.93 us
  transfers between devices with their start and end apart: 5, of which 4 were waited for; matrix products, arithmetic and copies ran while one was open for 0% of the time, Pallas kernels for 0%

profile of v5, /device:TPU:1, one launch (start us, length us, event | category | flops | bytes accessed | tf_op | source)
XLA Modules:
  0.0 75.0 jit_solution(8204187776302606637)
XLA Ops:
  0.0 2.0 %split.1 = bf16[16,128,256]{2,1,0:T(8,128)(2,1)} custom-call(bf16[1,128,4096]{2,1,0:T(8,128)(2,1)} %p_ref.1), custom_call_target="tpu_custom_call" | custom-call | tf_op jit(solution)/shard_map/split/pallas_call | solution.py:92
  2.0 0.0 copy-start.1
  2.1 7.8 %all-to-all-start = ((bf16[16,128,256]{2,1,0:T(8,128)(2,1)}), bf16[16,128,256]{2,1,0:T(8,128)(2,1)S(1)}, u32[]{:S(2)}, u32[]{:S(2)}) async-start(bf16[16,128,256]{2,1,0:T(8,128)(2,1)} %split.1), calls=%async_computation | async-start | bytes 2097152 | tf_op jit(solution)/shard_map/all_to_all | solution.py:161
  9.9 0.0 copy-done.1
  9.9 6.7 %collective-permute-start.1 = (bf16[128,128]{1,0:T(8,128)(2,1)S(1)}, bf16[128,128]{1,0:T(8,128)(2,1)S(1)}, u32[]{:S(2)}, u32[]{:S(2)}) collective-permute-start(bf16[128,128]{1,0:T(8,128)(2,1)S(1)} %copy-done.1), channel_id=1, source_target_pairs={{0,80},{64,10},{128,2},{192,15},{256,0},{320,8},{384,7},{448,88},{... | collective-permute-start | bytes 98312 | tf_op jit(solution)/shard_map/ppermute | solution.py:162
  16.6 5.9 %collective-permute-done.1 = bf16[128,128]{1,0:T(8,128)(2,1)S(1)} collective-permute-done((bf16[128,128]{1,0:T(8,128)(2,1)S(1)}, bf16[128,128]{1,0:T(8,128)(2,1)S(1)}, u32[]{:S(2)}, u32[]{:S(2)}) %collective-permute-start.1) | collective-permute-done | bytes 32800 | tf_op jit(solution)/shard_map/ppermute | solution.py:162
  22.5 0.4 all-to-all-done
  22.9 0.9 %broadcast_in_dim.2 = bf16[16,128,128]{2,1,0:T(8,128)(2,1)} broadcast(bf16[128,128]{1,0:T(8,128)(2,1)S(1)} %collective-permute-done.1), dimensions={1,2} | broadcast | bytes 557056 | tf_op jit(solution)/shard_map/broadcast_in_dim | solution.py:163
  23.8 18.5 %all-to-all-start.1 = ((bf16[16,128,128]{2,1,0:T(8,128)(2,1)}), bf16[16,128,128]{2,1,0:T(8,128)(2,1)S(1)}, u32[]{:S(2)}, u32[]{:S(2)}) async-start(bf16[16,128,128]{2,1,0:T(8,128)(2,1)} %broadcast_in_dim.2), calls=%async_computation.1 | async-start | bytes 1048576 | tf_op jit(solution)/shard_map/all_to_all | solution.py:164
  42.3 0.0 copy-start
  42.3 2.9 %collective-permute-start = (bf16[8,256,256]{2,1,0:T(8,128)(2,1)S(1)}, bf16[8,256,256]{2,1,0:T(8,128)(2,1)S(1)}, u32[]{:S(2)}, u32[]{:S(2)}) collective-permute-start(bf16[8,256,256]{2,1,0:T(8,128)(2,1)S(1)} %bitcast.1), channel_id=1, source_target_pairs={{0,32},{32,0},{1,33},{33,1},{2,34},{34,2},{3,35},{35,3},{4,36},{36... | collective-permute-start | bytes 3145736 | tf_op jit(solution)/shard_map/ppermute | solution.py:166
  45.2 10.1 %all-to-all-done.1.x_ref = bf16[16,128,128]{2,1,0:T(8,128)(2,1)S(1)} async-done(((bf16[16,128,128]{2,1,0:T(8,128)(2,1)}), bf16[16,128,128]{2,1,0:T(8,128)(2,1)S(1)}, u32[]{:S(2)}, u32[]{:S(2)}) %all-to-all-start.1) | async-done | bytes 524320 | tf_op jit(solution)/shard_map/all_to_all | solution.py:164
  55.3 3.4 %collective-permute-start.2 = (bf16[16,16,128]{2,1,0:T(8,128)(2,1)S(1)}, bf16[16,16,128]{2,1,0:T(8,128)(2,1)S(1)}, u32[]{:S(2)}, u32[]{:S(2)}) collective-permute-start(bf16[16,16,128]{2,1,0:T(8,128)(2,1)S(1)} %slice.4), channel_id=1, source_target_pairs={{0,32},{32,0},{1,33},{33,1},{2,34},{34,2},{3,35},{35,3},{4,36},{36... | collective-permute-start | bytes 196616 | tf_op jit(solution)/shard_map/ppermute | solution.py:165
  58.7 0.9 %collective-permute-done.2.h_ref = bf16[16,16,128]{2,1,0:T(8,128)(2,1)S(1)} collective-permute-done((bf16[16,16,128]{2,1,0:T(8,128)(2,1)S(1)}, bf16[16,16,128]{2,1,0:T(8,128)(2,1)S(1)}, u32[]{:S(2)}, u32[]{:S(2)}) %collective-permute-start.2) | collective-permute-done | bytes 65568 | tf_op jit(solution)/shard_map/ppermute | solution.py:165
  59.6 0.0 collective-permute-done.other_ref
  59.6 0.0 copy-done
  59.6 2.4 %field.1 = (f32[16,128,128]{2,1,0:T(8,128)S(1)}, f32[128,128]{1,0:T(8,128)S(1)}) custom-call(bf16[8,256,256]{2,1,0:T(8,128)(2,1)S(1)} %bitcast.2, bf16[8,256,256]{2,1,0:T(8,128)(2,1)S(1)} %collective-permute-done.other_ref, bf16[16,128,128]{2,1,0:T(8,128)(2,1)S(1)} %all-to-all-done.1.x_ref, bf16[16,16,128]{2,1,0:T(8,128)(2,1)S(1)} %collective-permute-done.2.h_ref, ...), custom_call_target="tpu_custom_call" | custom-call | tf_op jit(solution)/shard_map/field/pallas_call | solution.py:148
  62.0 0.1 convert_element_type.6
  62.1 12.2 %all_to_all.15 = f16[16,128,128]{2,1,0:T(8,128)(2,1)S(1)} all-to-all(f16[16,128,128]{2,1,0:T(8,128)(2,1)S(1)} %convert_element_type.6), channel_id=1, replica_groups=mesh['x'=4,'yl'=2,'c'=2,'yh'=4,'zh'=4,'zl'=2] {'x','yl','zl'}, dimensions={0} | all-to-all | bytes 1048576 | tf_op jit(solution)/shard_map/all_to_all | solution.py:168
  74.3 0.1 convert_reduce_fusion
  74.4 0.6 sub.3
  (1 shorter events, 0.0 us)
Async XLA Ops:
  2.0 7.8 %copy-start.1 = (bf16[128,128]{1,0:T(8,128)(2,1)S(1)}, bf16[128,128]{1,0:T(8,128)(2,1)}, u32[]{:S(2)}) copy-start(bf16[128,128]{1,0:T(8,128)(2,1)} %param.3) | copy-start | bytes 98308
  2.1 20.9 %all-to-all-start = ((bf16[16,128,256]{2,1,0:T(8,128)(2,1)}), bf16[16,128,256]{2,1,0:T(8,128)(2,1)S(1)}, u32[]{:S(2)}, u32[]{:S(2)}) async-start(bf16[16,128,256]{2,1,0:T(8,128)(2,1)} %split.1), calls=%async_computation | async-start | bytes 2097152 | tf_op jit(solution)/shard_map/all_to_all | solution.py:161
  9.9 12.6 %collective-permute-start.1 = (bf16[128,128]{1,0:T(8,128)(2,1)S(1)}, bf16[128,128]{1,0:T(8,128)(2,1)S(1)}, u32[]{:S(2)}, u32[]{:S(2)}) collective-permute-start(bf16[128,128]{1,0:T(8,128)(2,1)S(1)} %copy-done.1), channel_id=1, source_target_pairs={{0,80},{64,10},{128,2},{192,15},{256,0},{320,8},{384,7},{448,88},{... | collective-permute-start | bytes 98312 | tf_op jit(solution)/shard_map/ppermute | solution.py:162
  23.8 31.5 %all-to-all-start.1 = ((bf16[16,128,128]{2,1,0:T(8,128)(2,1)}), bf16[16,128,128]{2,1,0:T(8,128)(2,1)S(1)}, u32[]{:S(2)}, u32[]{:S(2)}) async-start(bf16[16,128,128]{2,1,0:T(8,128)(2,1)} %broadcast_in_dim.2), calls=%async_computation.1 | async-start | bytes 1048576 | tf_op jit(solution)/shard_map/all_to_all | solution.py:164
  42.3 17.3 %copy-start = (f32[128,128]{1,0:T(8,128)S(1)}, f32[128,128]{1,0:T(8,128)}, u32[]{:S(2)}) copy-start(f32[128,128]{1,0:T(8,128)} %e_ref.1) | copy-start | bytes 196612
  42.3 17.3 %collective-permute-start = (bf16[8,256,256]{2,1,0:T(8,128)(2,1)S(1)}, bf16[8,256,256]{2,1,0:T(8,128)(2,1)S(1)}, u32[]{:S(2)}, u32[]{:S(2)}) collective-permute-start(bf16[8,256,256]{2,1,0:T(8,128)(2,1)S(1)} %bitcast.1), channel_id=1, source_target_pairs={{0,32},{32,0},{1,33},{33,1},{2,34},{34,2},{3,35},{35,3},{4,36},{36... | collective-permute-start | bytes 3145736 | tf_op jit(solution)/shard_map/ppermute | solution.py:166
  55.3 4.3 %collective-permute-start.2 = (bf16[16,16,128]{2,1,0:T(8,128)(2,1)S(1)}, bf16[16,16,128]{2,1,0:T(8,128)(2,1)S(1)}, u32[]{:S(2)}, u32[]{:S(2)}) collective-permute-start(bf16[16,16,128]{2,1,0:T(8,128)(2,1)S(1)} %slice.4), channel_id=1, source_target_pairs={{0,32},{32,0},{1,33},{33,1},{2,34},{34,2},{3,35},{35,3},{4,36},{36... | collective-permute-start | bytes 196616 | tf_op jit(solution)/shard_map/ppermute | solution.py:165

commit v6 on v5

--- a/solution.py
+++ b/solution.py
@@ -37,7 +37,7 @@
 )
 
 
-ORDER = (11, 15, 10, 14, 7, 3, 6, 2, 9, 13, 5, 8, 1, 12, 4, 0)
+ORDER = (10, 14, 6, 2, 11, 15, 7, 3, 9, 13, 5, 1, 8, 12, 4, 0)
 
 
 def holder(s, c, piece):
@@ -63,6 +63,13 @@
     ]
 
 
+def trade_groups():
+    return [
+        [((x * 2 + yl) * 2 + c) * 32 + rows * 2 + zl for x in (3, 2, 1, 0) for yl in (1, 0) for zl in (1, 0)]
+        for c in range(2) for rows in range(16)
+    ]
+
+
 def split_kernel(p_ref, o_ref, in_ref, out_ref, in_sem, out_sem):
     parts = 4
     rows = B // parts
@@ -77,7 +84,7 @@
         for x in range(4):
             for qy in range(2):
                 for qz in range(2):
-                    to = x * 4 + ((qy * 2 + qz) ^ flip)
+                    to = 15 - (x * 4 + ((qy * 2 + qz) ^ flip))
                     for h in range(2):
                         col = SETS[x * 4 + qy * 2 + qz][h] * B
                         out_ref[to, here, h * B:(h + 1) * B] = in_ref[here, col:col + B]
@@ -134,10 +141,10 @@
         for k in range(LAGS):
             w_ref = own_ref if k % 2 == c else other_ref
             shifted = s_ref[:, HALO - k:HALO - k + B, :].astype(jnp.bfloat16).reshape(8 * B, 2 * B)
-            acc += lax.dot_general(shifted, w_ref[k // 2], (((1,), (1,)), ((), ())), preferred_element_type=jnp.float32)
+            acc += lax.dot_general(shifted, w_ref[7 - k // 2], (((1,), (1,)), ((), ())), preferred_element_type=jnp.float32)
         for m in range(8):
             for zl in range(2):
-                out_ref[m * 2 + zl] = acc[m * B:(m + 1) * B, zl * B:(zl + 1) * B]
+                out_ref[15 - m * 2 - zl] = acc[m * B:(m + 1) * B, (1 - zl) * B:(2 - zl) * B]
 
     pl.when(core == 0)(lambda: run(0))
     pl.when(core == 1)(lambda: run(1))
@@ -158,14 +165,14 @@
 
 def body(currents, panels, excitation):
     everyone = LAG + ROW
-    own = lax.all_to_all(split_panels(panels), TRADE, 0, 0, tiled=True).reshape(8, 2 * B, 2 * B)
+    own = lax.all_to_all(split_panels(panels), everyone, 0, 0, tiled=True, axis_index_groups=trade_groups()).reshape(8, 2 * B, 2 * B)
     block = lax.ppermute(currents, everyone, swap_pairs())
     copies = jnp.broadcast_to(block[None], (16,) + block.shape)
     x = lax.all_to_all(copies, everyone, 0, 0, tiled=True, axis_index_groups=copy_groups())
     ends = lax.ppermute(x[:, B - HALO:], "c", [(0, 1), (1, 0)])
     other = lax.ppermute(own, "c", [(0, 1), (1, 0)])
     part, kept = field_of(own, other, x, ends, excitation)
-    got = lax.all_to_all(part.astype(jnp.float16), TRADE, 0, 0, tiled=True)
+    got = lax.all_to_all(part.astype(jnp.float16), everyone, 0, 0, tiled=True, axis_index_groups=trade_groups())
     return kept - jnp.sum(got.astype(jnp.float32), 0)
 
 

time: 75.5 us -> 74.4 us (0.985)
  waiting for transfers between devices: 17.3 us -> 12.2 us
  starting transfers between devices: 39.3 us -> 41.6 us
  blocking collectives: 12.2 us -> 13.6 us
    all_to_all x1, waiting for transfers between devices: 10.1 us -> 5.92 us  [body(): lax.all_to_all(copies, everyone, 0, 0, tiled=True, axis_index_groups=copy...]
    ppermute x1, starting transfers between devices: 2.93 us -> 5.55 us  [body(): other = lax.ppermute(own, 'c', [(0, 1), (1, 0)])]
    all_to_all x1, starting transfers between devices: 18.5 us -> 16.2 us  [body(): lax.all_to_all(copies, everyone, 0, 0, tiled=True, axis_index_groups=copy...]
    all_to_all x1, starting transfers between devices: 7.79 us -> 9.68 us  [body(): lax.all_to_all(split_panels(panels), everyone, 0, 0, tiled=True, axis_ind...]
    all_to_all x1, blocking collectives: 12.2 us -> 13.6 us  [body(): lax.all_to_all(part.astype(jnp.float16), everyone, 0, 0, tiled=True, axis...]
    ppermute x1, starting transfers between devices: 3.38 us -> 4.5 us  [body(): ends = lax.ppermute(x[:, B - HALO:], 'c', [(0, 1), (1, 0)])]
    ppermute x1, starting transfers between devices: 6.73 us -> 5.64 us  [body(): block = lax.ppermute(currents, everyone, swap_pairs())]
  transfers between devices with their start and end apart: 5 -> 5, of which waited for: 4 -> 3; matrix products, arithmetic and copies ran while one was open for 0% -> 0% of each run, Pallas kernels for 0% -> 0%
where the time goes in v6:
time: 74.4 us; the launch traced here: 73.5 us
  starting transfers between devices  41.6 us (56%)
  blocking collectives  13.6 us (18%)
  waiting for transfers between devices  12.2 us (16%)
  Pallas kernels  4.45 us (6%)
  local copies, waits for them, and re-layouts  0.91 us (1%)
  other arithmetic  0.82 us (1%)
    all_to_all x1, starting transfers between devices, body(): lax.all_to_all(copies, everyone, 0, 0, tiled=True, axis_index_groups=copy...  16.2 us
    all_to_all x1, blocking collectives, body(): lax.all_to_all(part.astype(jnp.float16), everyone, 0, 0, tiled=True, axis...  13.6 us
    all_to_all x1, starting transfers between devices, body(): lax.all_to_all(split_panels(panels), everyone, 0, 0, tiled=True, axis_ind...  9.68 us
    all_to_all x1, waiting for transfers between devices, body(): lax.all_to_all(copies, everyone, 0, 0, tiled=True, axis_index_groups=copy...  5.92 us
    ppermute x1, starting transfers between devices, body(): block = lax.ppermute(currents, everyone, swap_pairs())  5.64 us
    ppermute x1, starting transfers between devices, body(): other = lax.ppermute(own, 'c', [(0, 1), (1, 0)])  5.55 us
    ppermute x1, waiting for transfers between devices, body(): block = lax.ppermute(currents, everyone, swap_pairs())  5.36 us
    ppermute x1, starting transfers between devices, body(): ends = lax.ppermute(x[:, B - HALO:], 'c', [(0, 1), (1, 0)])  4.5 us
  transfers between devices with their start and end apart: 5, of which 3 were waited for; matrix products, arithmetic and copies ran while one was open for 0% of the time, Pallas kernels for 0%

profile of v6, /device:TPU:1, one launch (start us, length us, event | category | flops | bytes accessed | tf_op | source)
XLA Modules:
  0.0 73.5 jit_solution(8802966857549907978)
XLA Ops:
  0.0 2.0 %split.1 = bf16[16,128,256]{2,1,0:T(8,128)(2,1)} custom-call(bf16[1,128,4096]{2,1,0:T(8,128)(2,1)} %p_ref.1), custom_call_target="tpu_custom_call" | custom-call | tf_op jit(solution)/shard_map/split/pallas_call | solution.py:99
  2.0 0.0 copy-start.1
  2.1 9.7 %all-to-all-start = ((bf16[16,128,256]{2,1,0:T(8,128)(2,1)}), bf16[16,128,256]{2,1,0:T(8,128)(2,1)S(1)}, u32[]{:S(2)}, u32[]{:S(2)}) async-start(bf16[16,128,256]{2,1,0:T(8,128)(2,1)} %split.1), calls=%async_computation | async-start | bytes 2097152 | tf_op jit(solution)/shard_map/all_to_all | solution.py:168
  11.7 0.0 copy-done.1
  11.7 5.6 %collective-permute-start.1 = (bf16[128,128]{1,0:T(8,128)(2,1)S(1)}, bf16[128,128]{1,0:T(8,128)(2,1)S(1)}, u32[]{:S(2)}, u32[]{:S(2)}) collective-permute-start(bf16[128,128]{1,0:T(8,128)(2,1)S(1)} %copy-done.1), channel_id=1, source_target_pairs={{0,80},{64,10},{128,2},{192,15},{256,0},{320,8},{384,7},{448,88},{... | collective-permute-start | bytes 98312 | tf_op jit(solution)/shard_map/ppermute | solution.py:169
  17.4 5.4 %collective-permute-done.1 = bf16[128,128]{1,0:T(8,128)(2,1)S(1)} collective-permute-done((bf16[128,128]{1,0:T(8,128)(2,1)S(1)}, bf16[128,128]{1,0:T(8,128)(2,1)S(1)}, u32[]{:S(2)}, u32[]{:S(2)}) %collective-permute-start.1) | collective-permute-done | bytes 32800 | tf_op jit(solution)/shard_map/ppermute | solution.py:169
  22.8 0.0 all-to-all-done
  22.8 0.9 %broadcast_in_dim.2 = bf16[16,128,128]{2,1,0:T(8,128)(2,1)} broadcast(bf16[128,128]{1,0:T(8,128)(2,1)S(1)} %collective-permute-done.1), dimensions={1,2} | broadcast | bytes 557056 | tf_op jit(solution)/shard_map/broadcast_in_dim | solution.py:170
  23.6 16.2 %all-to-all-start.1 = ((bf16[16,128,128]{2,1,0:T(8,128)(2,1)}), bf16[16,128,128]{2,1,0:T(8,128)(2,1)S(1)}, u32[]{:S(2)}, u32[]{:S(2)}) async-start(bf16[16,128,128]{2,1,0:T(8,128)(2,1)} %broadcast_in_dim.2), calls=%async_computation.1 | async-start | bytes 1048576 | tf_op jit(solution)/shard_map/all_to_all | solution.py:171
  39.8 0.0 copy-start
  39.8 5.6 %collective-permute-start = (bf16[8,256,256]{2,1,0:T(8,128)(2,1)S(1)}, bf16[8,256,256]{2,1,0:T(8,128)(2,1)S(1)}, u32[]{:S(2)}, u32[]{:S(2)}) collective-permute-start(bf16[8,256,256]{2,1,0:T(8,128)(2,1)S(1)} %bitcast.1), channel_id=1, source_target_pairs={{0,32},{32,0},{1,33},{33,1},{2,34},{34,2},{3,35},{35,3},{4,36},{36... | collective-permute-start | bytes 3145736 | tf_op jit(solution)/shard_map/ppermute | solution.py:173
  45.4 5.9 %all-to-all-done.1.x_ref = bf16[16,128,128]{2,1,0:T(8,128)(2,1)S(1)} async-done(((bf16[16,128,128]{2,1,0:T(8,128)(2,1)}), bf16[16,128,128]{2,1,0:T(8,128)(2,1)S(1)}, u32[]{:S(2)}, u32[]{:S(2)}) %all-to-all-start.1) | async-done | bytes 524320 | tf_op jit(solution)/shard_map/all_to_all | solution.py:171
  51.3 4.5 %collective-permute-start.2 = (bf16[16,16,128]{2,1,0:T(8,128)(2,1)S(1)}, bf16[16,16,128]{2,1,0:T(8,128)(2,1)S(1)}, u32[]{:S(2)}, u32[]{:S(2)}) collective-permute-start(bf16[16,16,128]{2,1,0:T(8,128)(2,1)S(1)} %slice.4), channel_id=1, source_target_pairs={{0,32},{32,0},{1,33},{33,1},{2,34},{34,2},{3,35},{35,3},{4,36},{36... | collective-permute-start | bytes 196616 | tf_op jit(solution)/shard_map/ppermute | solution.py:172
  55.8 0.9 %collective-permute-done.2.h_ref = bf16[16,16,128]{2,1,0:T(8,128)(2,1)S(1)} collective-permute-done((bf16[16,16,128]{2,1,0:T(8,128)(2,1)S(1)}, bf16[16,16,128]{2,1,0:T(8,128)(2,1)S(1)}, u32[]{:S(2)}, u32[]{:S(2)}) %collective-permute-start.2) | collective-permute-done | bytes 65568 | tf_op jit(solution)/shard_map/ppermute | solution.py:172
  56.7 0.0 collective-permute-done.other_ref
  56.7 0.0 copy-done
  56.7 2.4 %field.1 = (f32[16,128,128]{2,1,0:T(8,128)S(1)}, f32[128,128]{1,0:T(8,128)S(1)}) custom-call(bf16[8,256,256]{2,1,0:T(8,128)(2,1)S(1)} %bitcast.2, bf16[8,256,256]{2,1,0:T(8,128)(2,1)S(1)} %collective-permute-done.other_ref, bf16[16,128,128]{2,1,0:T(8,128)(2,1)S(1)} %all-to-all-done.1.x_ref, bf16[16,16,128]{2,1,0:T(8,128)(2,1)S(1)} %collective-permute-done.2.h_ref, ...), custom_call_target="tpu_custom_call" | custom-call | tf_op jit(solution)/shard_map/field/pallas_call | solution.py:155
  59.1 0.1 convert_element_type.6
  59.3 13.6 %all_to_all.15 = f16[16,128,128]{2,1,0:T(8,128)(2,1)S(1)} all-to-all(f16[16,128,128]{2,1,0:T(8,128)(2,1)S(1)} %convert_element_type.6), channel_id=1, replica_groups={{449,448,385,384,321,320,257,256,193,192,129,128,65,64,1,0},{451,450,38..., dimensions={0} | all-to-all | bytes 1048576 | tf_op jit(solution)/shard_map/all_to_all | solution.py:175
  72.8 0.1 convert_reduce_fusion
  72.9 0.6 sub.3
  (1 shorter events, 0.0 us)
Async XLA Ops:
  2.0 9.7 %copy-start.1 = (bf16[128,128]{1,0:T(8,128)(2,1)S(1)}, bf16[128,128]{1,0:T(8,128)(2,1)}, u32[]{:S(2)}) copy-start(bf16[128,128]{1,0:T(8,128)(2,1)} %param.3) | copy-start | bytes 98308
  2.1 20.7 %all-to-all-start = ((bf16[16,128,256]{2,1,0:T(8,128)(2,1)}), bf16[16,128,256]{2,1,0:T(8,128)(2,1)S(1)}, u32[]{:S(2)}, u32[]{:S(2)}) async-start(bf16[16,128,256]{2,1,0:T(8,128)(2,1)} %split.1), calls=%async_computation | async-start | bytes 2097152 | tf_op jit(solution)/shard_map/all_to_all | solution.py:168
  11.7 11.0 %collective-permute-start.1 = (bf16[128,128]{1,0:T(8,128)(2,1)S(1)}, bf16[128,128]{1,0:T(8,128)(2,1)S(1)}, u32[]{:S(2)}, u32[]{:S(2)}) collective-permute-start(bf16[128,128]{1,0:T(8,128)(2,1)S(1)} %copy-done.1), channel_id=1, source_target_pairs={{0,80},{64,10},{128,2},{192,15},{256,0},{320,8},{384,7},{448,88},{... | collective-permute-start | bytes 98312 | tf_op jit(solution)/shard_map/ppermute | solution.py:169
  23.6 27.7 %all-to-all-start.1 = ((bf16[16,128,128]{2,1,0:T(8,128)(2,1)}), bf16[16,128,128]{2,1,0:T(8,128)(2,1)S(1)}, u32[]{:S(2)}, u32[]{:S(2)}) async-start(bf16[16,128,128]{2,1,0:T(8,128)(2,1)} %broadcast_in_dim.2), calls=%async_computation.1 | async-start | bytes 1048576 | tf_op jit(solution)/shard_map/all_to_all | solution.py:171
  39.8 16.9 %copy-start = (f32[128,128]{1,0:T(8,128)S(1)}, f32[128,128]{1,0:T(8,128)}, u32[]{:S(2)}) copy-start(f32[128,128]{1,0:T(8,128)} %e_ref.1) | copy-start | bytes 196612
  39.8 16.9 %collective-permute-start = (bf16[8,256,256]{2,1,0:T(8,128)(2,1)S(1)}, bf16[8,256,256]{2,1,0:T(8,128)(2,1)S(1)}, u32[]{:S(2)}, u32[]{:S(2)}) collective-permute-start(bf16[8,256,256]{2,1,0:T(8,128)(2,1)S(1)} %bitcast.1), channel_id=1, source_target_pairs={{0,32},{32,0},{1,33},{33,1},{2,34},{34,2},{3,35},{35,3},{4,36},{36... | collective-permute-start | bytes 3145736 | tf_op jit(solution)/shard_map/ppermute | solution.py:173
  51.3 5.4 %collective-permute-start.2 = (bf16[16,16,128]{2,1,0:T(8,128)(2,1)S(1)}, bf16[16,16,128]{2,1,0:T(8,128)(2,1)S(1)}, u32[]{:S(2)}, u32[]{:S(2)}) collective-permute-start(bf16[16,16,128]{2,1,0:T(8,128)(2,1)S(1)} %slice.4), channel_id=1, source_target_pairs={{0,32},{32,0},{1,33},{33,1},{2,34},{34,2},{3,35},{35,3},{4,36},{36... | collective-permute-start | bytes 196616 | tf_op jit(solution)/shard_map/ppermute | solution.py:172

commit v7 on v6

--- a/solution.py
+++ b/solution.py
@@ -37,7 +37,10 @@
 )
 
 
-ORDER = (10, 14, 6, 2, 11, 15, 7, 3, 9, 13, 5, 1, 8, 12, 4, 0)
+ORDERS = (
+    (10, 14, 6, 2, 11, 15, 7, 3, 9, 13, 5, 1, 8, 12, 4, 0),
+    (14, 10, 2, 6, 15, 11, 3, 7, 13, 9, 1, 5, 12, 8, 0, 4),
+)
 
 
 def holder(s, c, piece):
@@ -48,11 +51,11 @@
 
 
 def copy_groups():
-    return [[holder(s, c, HOLDS[s].index(spot)) for spot in ORDER] for s in range(16) for c in range(2)]
+    return [[holder(s, c, HOLDS[s].index(spot)) for spot in ORDERS[s // 2 % 2]] for s in range(16) for c in range(2)]
 
 
-def packed(places):
-    word = sum(ORDER.index(place) << 4 * i for i, place in enumerate(places))
+def packed(s, places):
+    word = sum(ORDERS[s // 2 % 2].index(place) << 4 * i for i, place in enumerate(places))
     return word - (1 << 32) if word >= 1 << 31 else word
 
 
@@ -121,7 +124,7 @@
     for h in range(2):
         word = jnp.int32(0)
         for s in range(16):
-            word = jnp.where(mine == s, jnp.int32(packed(HOLDS[s][h * 8:h * 8 + 8])), word)
+            word = jnp.where(mine == s, jnp.int32(packed(s, HOLDS[s][h * 8:h * 8 + 8])), word)
         words.append(word)
 
     def place(m, h):

time: 74.4 us -> 75.3 us (1.012)
  blocking collectives: 13.6 us -> 15.2 us
  starting transfers between devices: 41.6 us -> 40.2 us
    all_to_all x1, blocking collectives: 13.6 us -> 15.2 us  [body(): lax.all_to_all(part.astype(jnp.float16), everyone, 0, 0, tiled=True, axis...]
    ppermute x1, starting transfers between devices: 4.5 us -> 3.19 us  [body(): ends = lax.ppermute(x[:, B - HALO:], 'c', [(0, 1), (1, 0)])]
where the time goes in v7:
time: 75.3 us; the launch traced here: 74.4 us
  starting transfers between devices  40.2 us (53%)
  blocking collectives  15.2 us (20%)
  waiting for transfers between devices  12.8 us (17%)
  Pallas kernels  4.45 us (6%)
  local copies, waits for them, and re-layouts  0.91 us (1%)
  other arithmetic  0.82 us (1%)
    all_to_all x1, starting transfers between devices, body(): lax.all_to_all(copies, everyone, 0, 0, tiled=True, axis_index_groups=copy...  16.2 us
    all_to_all x1, blocking collectives, body(): lax.all_to_all(part.astype(jnp.float16), everyone, 0, 0, tiled=True, axis...  15.2 us
    all_to_all x1, starting transfers between devices, body(): lax.all_to_all(split_panels(panels), everyone, 0, 0, tiled=True, axis_ind...  9.68 us
    all_to_all x1, waiting for transfers between devices, body(): lax.all_to_all(copies, everyone, 0, 0, tiled=True, axis_index_groups=copy...  6.51 us
    ppermute x1, starting transfers between devices, body(): block = lax.ppermute(currents, everyone, swap_pairs())  5.64 us
    ppermute x1, starting transfers between devices, body(): other = lax.ppermute(own, 'c', [(0, 1), (1, 0)])  5.55 us
    ppermute x1, waiting for transfers between devices, body(): block = lax.ppermute(currents, everyone, swap_pairs())  5.36 us
    ppermute x1, starting transfers between devices, body(): ends = lax.ppermute(x[:, B - HALO:], 'c', [(0, 1), (1, 0)])  3.19 us
  transfers between devices with their start and end apart: 5, of which 3 were waited for; matrix products, arithmetic and copies ran while one was open for 0% of the time, Pallas kernels for 0%

profile of v7, /device:TPU:1, one launch (start us, length us, event | category | flops | bytes accessed | tf_op | source)
XLA Modules:
  0.0 74.4 jit_solution(11091188198310010971)
XLA Ops:
  0.0 2.0 %split.1 = bf16[16,128,256]{2,1,0:T(8,128)(2,1)} custom-call(bf16[1,128,4096]{2,1,0:T(8,128)(2,1)} %p_ref.1), custom_call_target="tpu_custom_call" | custom-call | tf_op jit(solution)/shard_map/split/pallas_call | solution.py:102
  2.0 0.0 copy-start.1
  2.1 9.7 %all-to-all-start = ((bf16[16,128,256]{2,1,0:T(8,128)(2,1)}), bf16[16,128,256]{2,1,0:T(8,128)(2,1)S(1)}, u32[]{:S(2)}, u32[]{:S(2)}) async-start(bf16[16,128,256]{2,1,0:T(8,128)(2,1)} %split.1), calls=%async_computation | async-start | bytes 2097152 | tf_op jit(solution)/shard_map/all_to_all | solution.py:171
  11.7 0.0 copy-done.1
  11.7 5.6 %collective-permute-start.1 = (bf16[128,128]{1,0:T(8,128)(2,1)S(1)}, bf16[128,128]{1,0:T(8,128)(2,1)S(1)}, u32[]{:S(2)}, u32[]{:S(2)}) collective-permute-start(bf16[128,128]{1,0:T(8,128)(2,1)S(1)} %copy-done.1), channel_id=1, source_target_pairs={{0,80},{64,10},{128,2},{192,15},{256,0},{320,8},{384,7},{448,88},{... | collective-permute-start | bytes 98312 | tf_op jit(solution)/shard_map/ppermute | solution.py:172
  17.4 5.4 %collective-permute-done.1 = bf16[128,128]{1,0:T(8,128)(2,1)S(1)} collective-permute-done((bf16[128,128]{1,0:T(8,128)(2,1)S(1)}, bf16[128,128]{1,0:T(8,128)(2,1)S(1)}, u32[]{:S(2)}, u32[]{:S(2)}) %collective-permute-start.1) | collective-permute-done | bytes 32800 | tf_op jit(solution)/shard_map/ppermute | solution.py:172
  22.8 0.0 all-to-all-done
  22.8 0.9 %broadcast_in_dim.2 = bf16[16,128,128]{2,1,0:T(8,128)(2,1)} broadcast(bf16[128,128]{1,0:T(8,128)(2,1)S(1)} %collective-permute-done.1), dimensions={1,2} | broadcast | bytes 557056 | tf_op jit(solution)/shard_map/broadcast_in_dim | solution.py:173
  23.6 16.2 %all-to-all-start.1 = ((bf16[16,128,128]{2,1,0:T(8,128)(2,1)}), bf16[16,128,128]{2,1,0:T(8,128)(2,1)S(1)}, u32[]{:S(2)}, u32[]{:S(2)}) async-start(bf16[16,128,128]{2,1,0:T(8,128)(2,1)} %broadcast_in_dim.2), calls=%async_computation.1 | async-start | bytes 1048576 | tf_op jit(solution)/shard_map/all_to_all | solution.py:174
  39.8 0.0 copy-start
  39.8 5.6 %collective-permute-start = (bf16[8,256,256]{2,1,0:T(8,128)(2,1)S(1)}, bf16[8,256,256]{2,1,0:T(8,128)(2,1)S(1)}, u32[]{:S(2)}, u32[]{:S(2)}) collective-permute-start(bf16[8,256,256]{2,1,0:T(8,128)(2,1)S(1)} %bitcast.1), channel_id=1, source_target_pairs={{0,32},{32,0},{1,33},{33,1},{2,34},{34,2},{3,35},{35,3},{4,36},{36... | collective-permute-start | bytes 3145736 | tf_op jit(solution)/shard_map/ppermute | solution.py:176
  45.4 6.5 %all-to-all-done.1.x_ref = bf16[16,128,128]{2,1,0:T(8,128)(2,1)S(1)} async-done(((bf16[16,128,128]{2,1,0:T(8,128)(2,1)}), bf16[16,128,128]{2,1,0:T(8,128)(2,1)S(1)}, u32[]{:S(2)}, u32[]{:S(2)}) %all-to-all-start.1) | async-done | bytes 524320 | tf_op jit(solution)/shard_map/all_to_all | solution.py:174
  51.9 3.2 %collective-permute-start.2 = (bf16[16,16,128]{2,1,0:T(8,128)(2,1)S(1)}, bf16[16,16,128]{2,1,0:T(8,128)(2,1)S(1)}, u32[]{:S(2)}, u32[]{:S(2)}) collective-permute-start(bf16[16,16,128]{2,1,0:T(8,128)(2,1)S(1)} %slice.4), channel_id=1, source_target_pairs={{0,32},{32,0},{1,33},{33,1},{2,34},{34,2},{3,35},{35,3},{4,36},{36... | collective-permute-start | bytes 196616 | tf_op jit(solution)/shard_map/ppermute | solution.py:175
  55.1 0.9 %collective-permute-done.2.h_ref = bf16[16,16,128]{2,1,0:T(8,128)(2,1)S(1)} collective-permute-done((bf16[16,16,128]{2,1,0:T(8,128)(2,1)S(1)}, bf16[16,16,128]{2,1,0:T(8,128)(2,1)S(1)}, u32[]{:S(2)}, u32[]{:S(2)}) %collective-permute-start.2) | collective-permute-done | bytes 65568 | tf_op jit(solution)/shard_map/ppermute | solution.py:175
  56.0 0.0 collective-permute-done.other_ref
  56.0 0.0 copy-done
  56.0 2.4 %field.1 = (f32[16,128,128]{2,1,0:T(8,128)S(1)}, f32[128,128]{1,0:T(8,128)S(1)}) custom-call(bf16[8,256,256]{2,1,0:T(8,128)(2,1)S(1)} %bitcast.2, bf16[8,256,256]{2,1,0:T(8,128)(2,1)S(1)} %collective-permute-done.other_ref, bf16[16,128,128]{2,1,0:T(8,128)(2,1)S(1)} %all-to-all-done.1.x_ref, bf16[16,16,128]{2,1,0:T(8,128)(2,1)S(1)} %collective-permute-done.2.h_ref, ...), custom_call_target="tpu_custom_call" | custom-call | tf_op jit(solution)/shard_map/field/pallas_call | solution.py:158
  58.4 0.1 convert_element_type.6
  58.5 15.2 %all_to_all.15 = f16[16,128,128]{2,1,0:T(8,128)(2,1)S(1)} all-to-all(f16[16,128,128]{2,1,0:T(8,128)(2,1)S(1)} %convert_element_type.6), channel_id=1, replica_groups={{449,448,385,384,321,320,257,256,193,192,129,128,65,64,1,0},{451,450,38..., dimensions={0} | all-to-all | bytes 1048576 | tf_op jit(solution)/shard_map/all_to_all | solution.py:178
  73.7 0.1 convert_reduce_fusion
  73.8 0.6 sub.3
  (1 shorter events, 0.0 us)
Async XLA Ops:
  2.0 9.7 %copy-start.1 = (bf16[128,128]{1,0:T(8,128)(2,1)S(1)}, bf16[128,128]{1,0:T(8,128)(2,1)}, u32[]{:S(2)}) copy-start(bf16[128,128]{1,0:T(8,128)(2,1)} %param.3) | copy-start | bytes 98308
  2.1 20.7 %all-to-all-start = ((bf16[16,128,256]{2,1,0:T(8,128)(2,1)}), bf16[16,128,256]{2,1,0:T(8,128)(2,1)S(1)}, u32[]{:S(2)}, u32[]{:S(2)}) async-start(bf16[16,128,256]{2,1,0:T(8,128)(2,1)} %split.1), calls=%async_computation | async-start | bytes 2097152 | tf_op jit(solution)/shard_map/all_to_all | solution.py:171
  11.7 11.0 %collective-permute-start.1 = (bf16[128,128]{1,0:T(8,128)(2,1)S(1)}, bf16[128,128]{1,0:T(8,128)(2,1)S(1)}, u32[]{:S(2)}, u32[]{:S(2)}) collective-permute-start(bf16[128,128]{1,0:T(8,128)(2,1)S(1)} %copy-done.1), channel_id=1, source_target_pairs={{0,80},{64,10},{128,2},{192,15},{256,0},{320,8},{384,7},{448,88},{... | collective-permute-start | bytes 98312 | tf_op jit(solution)/shard_map/ppermute | solution.py:172
  23.6 28.3 %all-to-all-start.1 = ((bf16[16,128,128]{2,1,0:T(8,128)(2,1)}), bf16[16,128,128]{2,1,0:T(8,128)(2,1)S(1)}, u32[]{:S(2)}, u32[]{:S(2)}) async-start(bf16[16,128,128]{2,1,0:T(8,128)(2,1)} %broadcast_in_dim.2), calls=%async_computation.1 | async-start | bytes 1048576 | tf_op jit(solution)/shard_map/all_to_all | solution.py:174
  39.8 16.2 %copy-start = (f32[128,128]{1,0:T(8,128)S(1)}, f32[128,128]{1,0:T(8,128)}, u32[]{:S(2)}) copy-start(f32[128,128]{1,0:T(8,128)} %e_ref.1) | copy-start | bytes 196612
  39.8 16.2 %collective-permute-start = (bf16[8,256,256]{2,1,0:T(8,128)(2,1)S(1)}, bf16[8,256,256]{2,1,0:T(8,128)(2,1)S(1)}, u32[]{:S(2)}, u32[]{:S(2)}) collective-permute-start(bf16[8,256,256]{2,1,0:T(8,128)(2,1)S(1)} %bitcast.1), channel_id=1, source_target_pairs={{0,32},{32,0},{1,33},{33,1},{2,34},{34,2},{3,35},{35,3},{4,36},{36... | collective-permute-start | bytes 3145736 | tf_op jit(solution)/shard_map/ppermute | solution.py:176
  51.9 4.1 %collective-permute-start.2 = (bf16[16,16,128]{2,1,0:T(8,128)(2,1)S(1)}, bf16[16,16,128]{2,1,0:T(8,128)(2,1)S(1)}, u32[]{:S(2)}, u32[]{:S(2)}) collective-permute-start(bf16[16,16,128]{2,1,0:T(8,128)(2,1)S(1)} %slice.4), channel_id=1, source_target_pairs={{0,32},{32,0},{1,33},{33,1},{2,34},{34,2},{3,35},{35,3},{4,36},{36... | collective-permute-start | bytes 196616 | tf_op jit(solution)/shard_map/ppermute | solution.py:175

commit v8 on v6

--- a/solution.py
+++ b/solution.py
@@ -71,7 +71,7 @@
 
 
 def split_kernel(p_ref, o_ref, in_ref, out_ref, in_sem, out_sem):
-    parts = 4
+    parts = 8
     rows = B // parts
     loads = [pltpu.make_async_copy(p_ref.at[0, pl.ds(i * rows, rows)], in_ref.at[pl.ds(i * rows, rows)], in_sem.at[i]) for i in range(parts)]
     for load in loads:
@@ -104,8 +104,8 @@
         scratch_shapes=[
             pltpu.VMEM((B, 32 * B), jnp.bfloat16),
             pltpu.VMEM((16, B, 2 * B), jnp.bfloat16),
-            pltpu.SemaphoreType.DMA((4,)),
-            pltpu.SemaphoreType.DMA((4,)),
+            pltpu.SemaphoreType.DMA((8,)),
+            pltpu.SemaphoreType.DMA((8,)),
         ],
         name="split",
     )(panels)

time: 74.4 us -> 74.5 us (level)
  no operation moved by 1% of the time
where the time goes in v8:
time: 74.5 us; the launch traced here: 73.6 us
  starting transfers between devices  41.6 us (56%)
  blocking collectives  13.6 us (18%)
  waiting for transfers between devices  12.2 us (16%)
  Pallas kernels  4.53 us (6%)
  local copies, waits for them, and re-layouts  0.91 us (1%)
  other arithmetic  0.82 us (1%)
    all_to_all x1, starting transfers between devices, body(): lax.all_to_all(copies, everyone, 0, 0, tiled=True, axis_index_groups=copy...  16.2 us
    all_to_all x1, blocking collectives, body(): lax.all_to_all(part.astype(jnp.float16), everyone, 0, 0, tiled=True, axis...  13.6 us
    all_to_all x1, starting transfers between devices, body(): lax.all_to_all(split_panels(panels), everyone, 0, 0, tiled=True, axis_ind...  9.68 us
    all_to_all x1, waiting for transfers between devices, body(): lax.all_to_all(copies, everyone, 0, 0, tiled=True, axis_index_groups=copy...  5.92 us
    ppermute x1, starting transfers between devices, body(): block = lax.ppermute(currents, everyone, swap_pairs())  5.64 us
    ppermute x1, starting transfers between devices, body(): other = lax.ppermute(own, 'c', [(0, 1), (1, 0)])  5.55 us
    ppermute x1, waiting for transfers between devices, body(): block = lax.ppermute(currents, everyone, swap_pairs())  5.36 us
    ppermute x1, starting transfers between devices, body(): ends = lax.ppermute(x[:, B - HALO:], 'c', [(0, 1), (1, 0)])  4.5 us
  transfers between devices with their start and end apart: 5, of which 3 were waited for; matrix products, arithmetic and copies ran while one was open for 0% of the time, Pallas kernels for 0%

profile of v8, /device:TPU:1, one launch (start us, length us, event | category | flops | bytes accessed | tf_op | source)
XLA Modules:
  0.0 73.6 jit_solution(1805744896720153221)
XLA Ops:
  0.0 2.1 %split.1 = bf16[16,128,256]{2,1,0:T(8,128)(2,1)} custom-call(bf16[1,128,4096]{2,1,0:T(8,128)(2,1)} %p_ref.1), custom_call_target="tpu_custom_call" | custom-call | tf_op jit(solution)/shard_map/split/pallas_call | solution.py:99
  2.1 0.0 copy-start.1
  2.1 9.7 %all-to-all-start = ((bf16[16,128,256]{2,1,0:T(8,128)(2,1)}), bf16[16,128,256]{2,1,0:T(8,128)(2,1)S(1)}, u32[]{:S(2)}, u32[]{:S(2)}) async-start(bf16[16,128,256]{2,1,0:T(8,128)(2,1)} %split.1), calls=%async_computation | async-start | bytes 2097152 | tf_op jit(solution)/shard_map/all_to_all | solution.py:168
  11.8 0.0 copy-done.1
  11.8 5.6 %collective-permute-start.1 = (bf16[128,128]{1,0:T(8,128)(2,1)S(1)}, bf16[128,128]{1,0:T(8,128)(2,1)S(1)}, u32[]{:S(2)}, u32[]{:S(2)}) collective-permute-start(bf16[128,128]{1,0:T(8,128)(2,1)S(1)} %copy-done.1), channel_id=1, source_target_pairs={{0,80},{64,10},{128,2},{192,15},{256,0},{320,8},{384,7},{448,88},{... | collective-permute-start | bytes 98312 | tf_op jit(solution)/shard_map/ppermute | solution.py:169
  17.5 5.4 %collective-permute-done.1 = bf16[128,128]{1,0:T(8,128)(2,1)S(1)} collective-permute-done((bf16[128,128]{1,0:T(8,128)(2,1)S(1)}, bf16[128,128]{1,0:T(8,128)(2,1)S(1)}, u32[]{:S(2)}, u32[]{:S(2)}) %collective-permute-start.1) | collective-permute-done | bytes 32800 | tf_op jit(solution)/shard_map/ppermute | solution.py:169
  22.8 0.0 all-to-all-done
  22.8 0.9 %broadcast_in_dim.2 = bf16[16,128,128]{2,1,0:T(8,128)(2,1)} broadcast(bf16[128,128]{1,0:T(8,128)(2,1)S(1)} %collective-permute-done.1), dimensions={1,2} | broadcast | bytes 557056 | tf_op jit(solution)/shard_map/broadcast_in_dim | solution.py:170
  23.7 16.2 %all-to-all-start.1 = ((bf16[16,128,128]{2,1,0:T(8,128)(2,1)}), bf16[16,128,128]{2,1,0:T(8,128)(2,1)S(1)}, u32[]{:S(2)}, u32[]{:S(2)}) async-start(bf16[16,128,128]{2,1,0:T(8,128)(2,1)} %broadcast_in_dim.2), calls=%async_computation.1 | async-start | bytes 1048576 | tf_op jit(solution)/shard_map/all_to_all | solution.py:171
  39.9 0.0 copy-start
  39.9 5.6 %collective-permute-start = (bf16[8,256,256]{2,1,0:T(8,128)(2,1)S(1)}, bf16[8,256,256]{2,1,0:T(8,128)(2,1)S(1)}, u32[]{:S(2)}, u32[]{:S(2)}) collective-permute-start(bf16[8,256,256]{2,1,0:T(8,128)(2,1)S(1)} %bitcast.1), channel_id=1, source_target_pairs={{0,32},{32,0},{1,33},{33,1},{2,34},{34,2},{3,35},{35,3},{4,36},{36... | collective-permute-start | bytes 3145736 | tf_op jit(solution)/shard_map/ppermute | solution.py:173
  45.5 5.9 %all-to-all-done.1.x_ref = bf16[16,128,128]{2,1,0:T(8,128)(2,1)S(1)} async-done(((bf16[16,128,128]{2,1,0:T(8,128)(2,1)}), bf16[16,128,128]{2,1,0:T(8,128)(2,1)S(1)}, u32[]{:S(2)}, u32[]{:S(2)}) %all-to-all-start.1) | async-done | bytes 524320 | tf_op jit(solution)/shard_map/all_to_all | solution.py:171
  51.4 4.5 %collective-permute-start.2 = (bf16[16,16,128]{2,1,0:T(8,128)(2,1)S(1)}, bf16[16,16,128]{2,1,0:T(8,128)(2,1)S(1)}, u32[]{:S(2)}, u32[]{:S(2)}) collective-permute-start(bf16[16,16,128]{2,1,0:T(8,128)(2,1)S(1)} %slice.4), channel_id=1, source_target_pairs={{0,32},{32,0},{1,33},{33,1},{2,34},{34,2},{3,35},{35,3},{4,36},{36... | collective-permute-start | bytes 196616 | tf_op jit(solution)/shard_map/ppermute | solution.py:172
  55.9 0.9 %collective-permute-done.2.h_ref = bf16[16,16,128]{2,1,0:T(8,128)(2,1)S(1)} collective-permute-done((bf16[16,16,128]{2,1,0:T(8,128)(2,1)S(1)}, bf16[16,16,128]{2,1,0:T(8,128)(2,1)S(1)}, u32[]{:S(2)}, u32[]{:S(2)}) %collective-permute-start.2) | collective-permute-done | bytes 65568 | tf_op jit(solution)/shard_map/ppermute | solution.py:172
  56.8 0.0 collective-permute-done.other_ref
  56.8 0.0 copy-done
  56.8 2.4 %field.1 = (f32[16,128,128]{2,1,0:T(8,128)S(1)}, f32[128,128]{1,0:T(8,128)S(1)}) custom-call(bf16[8,256,256]{2,1,0:T(8,128)(2,1)S(1)} %bitcast.2, bf16[8,256,256]{2,1,0:T(8,128)(2,1)S(1)} %collective-permute-done.other_ref, bf16[16,128,128]{2,1,0:T(8,128)(2,1)S(1)} %all-to-all-done.1.x_ref, bf16[16,16,128]{2,1,0:T(8,128)(2,1)S(1)} %collective-permute-done.2.h_ref, ...), custom_call_target="tpu_custom_call" | custom-call | tf_op jit(solution)/shard_map/field/pallas_call | solution.py:155
  59.2 0.1 convert_element_type.6
  59.3 13.6 %all_to_all.15 = f16[16,128,128]{2,1,0:T(8,128)(2,1)S(1)} all-to-all(f16[16,128,128]{2,1,0:T(8,128)(2,1)S(1)} %convert_element_type.6), channel_id=1, replica_groups={{449,448,385,384,321,320,257,256,193,192,129,128,65,64,1,0},{451,450,38..., dimensions={0} | all-to-all | bytes 1048576 | tf_op jit(solution)/shard_map/all_to_all | solution.py:175
  72.9 0.1 convert_reduce_fusion
  73.0 0.6 sub.3
  (1 shorter events, 0.0 us)
Async XLA Ops:
  2.1 9.7 %copy-start.1 = (bf16[128,128]{1,0:T(8,128)(2,1)S(1)}, bf16[128,128]{1,0:T(8,128)(2,1)}, u32[]{:S(2)}) copy-start(bf16[128,128]{1,0:T(8,128)(2,1)} %param.3) | copy-start | bytes 98308
  2.1 20.7 %all-to-all-start = ((bf16[16,128,256]{2,1,0:T(8,128)(2,1)}), bf16[16,128,256]{2,1,0:T(8,128)(2,1)S(1)}, u32[]{:S(2)}, u32[]{:S(2)}) async-start(bf16[16,128,256]{2,1,0:T(8,128)(2,1)} %split.1), calls=%async_computation | async-start | bytes 2097152 | tf_op jit(solution)/shard_map/all_to_all | solution.py:168
  11.8 11.0 %collective-permute-start.1 = (bf16[128,128]{1,0:T(8,128)(2,1)S(1)}, bf16[128,128]{1,0:T(8,128)(2,1)S(1)}, u32[]{:S(2)}, u32[]{:S(2)}) collective-permute-start(bf16[128,128]{1,0:T(8,128)(2,1)S(1)} %copy-done.1), channel_id=1, source_target_pairs={{0,80},{64,10},{128,2},{192,15},{256,0},{320,8},{384,7},{448,88},{... | collective-permute-start | bytes 98312 | tf_op jit(solution)/shard_map/ppermute | solution.py:169
  23.7 27.7 %all-to-all-start.1 = ((bf16[16,128,128]{2,1,0:T(8,128)(2,1)}), bf16[16,128,128]{2,1,0:T(8,128)(2,1)S(1)}, u32[]{:S(2)}, u32[]{:S(2)}) async-start(bf16[16,128,128]{2,1,0:T(8,128)(2,1)} %broadcast_in_dim.2), calls=%async_computation.1 | async-start | bytes 1048576 | tf_op jit(solution)/shard_map/all_to_all | solution.py:171
  39.9 16.9 %copy-start = (f32[128,128]{1,0:T(8,128)S(1)}, f32[128,128]{1,0:T(8,128)}, u32[]{:S(2)}) copy-start(f32[128,128]{1,0:T(8,128)} %e_ref.1) | copy-start | bytes 196612
  39.9 16.9 %collective-permute-start = (bf16[8,256,256]{2,1,0:T(8,128)(2,1)S(1)}, bf16[8,256,256]{2,1,0:T(8,128)(2,1)S(1)}, u32[]{:S(2)}, u32[]{:S(2)}) collective-permute-start(bf16[8,256,256]{2,1,0:T(8,128)(2,1)S(1)} %bitcast.1), channel_id=1, source_target_pairs={{0,32},{32,0},{1,33},{33,1},{2,34},{34,2},{3,35},{35,3},{4,36},{36... | collective-permute-start | bytes 3145736 | tf_op jit(solution)/shard_map/ppermute | solution.py:173
  51.4 5.4 %collective-permute-start.2 = (bf16[16,16,128]{2,1,0:T(8,128)(2,1)S(1)}, bf16[16,16,128]{2,1,0:T(8,128)(2,1)S(1)}, u32[]{:S(2)}, u32[]{:S(2)}) collective-permute-start(bf16[16,16,128]{2,1,0:T(8,128)(2,1)S(1)} %slice.4), channel_id=1, source_target_pairs={{0,32},{32,0},{1,33},{33,1},{2,34},{34,2},{3,35},{35,3},{4,36},{36... | collective-permute-start | bytes 196616 | tf_op jit(solution)/shard_map/ppermute | solution.py:172
